TPU v7x, 256 devices: a whole 4x4x8 slice. The times are simulated.
256 devices in a mesh: seq: 16 (over x, y), nbr: 16 (over z, core).
Axes of the slice: x: 4, y: 4, z: 8, core: 2. Of those that a mesh axis runs over, the one named last changes fastest.
Arguments:
- tokens: bfloat16 [8192, 4096], P(('seq', 'nbr')), may hold values from -7 to 7
- nbr_embed: bfloat16 [256, 128, 896], P('seq', 'nbr'), may hold values from -7 to 7
- neighbour_table: int32 [128, 2], P('seq'), may hold values from 0 to 255, as said below
- valid_counts: int32 [128], replicated, may hold values from 1 to 2
- dec_proj: bfloat16 [4096, 3, 4096], P(None, None, 'nbr'), may hold values from -1 to 1
- enc_query: bfloat16 [896, 4096], P(None, 'nbr'), may hold values from -2 to 2
- enc_out: bfloat16 [4096, 896], P('nbr'), may hold values from -0.09375 to 0.09375
- enc_gain: float32 [896], replicated, may hold values from 0.1 to 1.9
- nbr_proj: bfloat16 [896, 2, 4096], P(None, None, 'nbr'), may hold values from -2 to 2
- out_proj: bfloat16 [4096, 4096], P('nbr'), may hold values from -0.09375 to 0.09375
Outputs:
- cross_out: bfloat16 [8192, 4096], P(('seq', 'nbr'))
- encoded: bfloat16 [32768, 896], P(('seq', 'nbr'))
Inputs may be any that keep to these rules, and one draw needn't show every extreme that they name: `neighbour_table`: for each block b of 8 groups in order, the entries of those groups are a permutation of the neighbour rows b * 16 to (b + 1) * 16 - 1.
All inputs are finite; a program needn't handle non-finite values.
Results may differ from a plain program's by a relative error of at most 0.025.
Values may be sent and summed in bfloat16 or wider, within the bound.
A program may use at most 128 MiB of HBM per device.

v0:
```python
import jax
import jax.numpy as jnp
from jax import lax
from jax.sharding import PartitionSpec as P

HEAD_DIM = 128
GROUP = 64
NLEN = 128
SEQ_LEN = 2048


def passed_along(block, axis, distance):
    devices = range(lax.axis_size(axis))
    route = [(i - distance, i) for i in devices if i - distance in devices]
    return lax.ppermute(block, axis, route)


def plain_softmax(scores):
    peak = jnp.max(scores, axis=-1, keepdims=True)
    raised = jnp.exp(scores - peak)
    return (raised / jnp.sum(raised, axis=-1, keepdims=True)).astype(jnp.bfloat16)


def masked_softmax(scores, allowed):
    live = jnp.any(allowed, axis=-1, keepdims=True)
    peak = jnp.max(jnp.where(allowed, scores, -1e30), axis=-1, keepdims=True)
    peak = jnp.where(live, peak, 0.0)
    raised = jnp.where(allowed, jnp.exp(scores - peak), 0.0)
    denominator = jnp.where(live, jnp.sum(raised, axis=-1, keepdims=True), 1.0)
    return (raised / denominator).astype(jnp.bfloat16)


def normed_rows(raw_rows, partial_sum, enc_gain):
    combined = raw_rows.astype(jnp.float32) + partial_sum
    factor = lax.rsqrt(jnp.mean(combined * combined, axis=-1, keepdims=True) + 1e-06)
    return (combined * factor * enc_gain).astype(jnp.bfloat16)


def local(
    tokens,
    nbr_embed,
    neighbour_table,
    valid_counts,
    dec_proj,
    enc_query,
    enc_out,
    enc_gain,
    nbr_proj,
    out_proj,
):
    n_nbr = lax.axis_size("nbr")
    seq_index = lax.axis_index("seq")
    member = lax.axis_index("nbr")
    model_width = tokens.shape[1]
    local_width = dec_proj.shape[2]
    head_dev = local_width // HEAD_DIM
    scale = 1.0 / HEAD_DIM**0.5
    dec_flat = dec_proj.reshape(model_width, 3 * local_width)
    projected = jnp.dot(
        lax.all_gather(tokens, "nbr", axis=0, tiled=True),
        dec_flat,
        preferred_element_type=jnp.float32,
    ).astype(jnp.bfloat16)
    tok_grp = projected.shape[0]
    ch_grp = tok_grp // GROUP
    queries = projected[:, :local_width]
    cond_key = projected[:, local_width : 2 * local_width].reshape(
        ch_grp, GROUP, head_dev, HEAD_DIM
    )
    cond_value = projected[:, 2 * local_width :].reshape(ch_grp, GROUP, head_dev, HEAD_DIM)
    grp_embed = lax.all_gather(nbr_embed, "nbr", axis=1, tiled=True)
    nb_grp = grp_embed.shape[0]
    enc_width = grp_embed.shape[2]
    row_ids = neighbour_table.reshape(-1) - seq_index * nb_grp
    ordered = jnp.take(grp_embed, row_ids, axis=0).reshape(-1, enc_width)
    enc_queries = jnp.dot(ordered, enc_query, preferred_element_type=jnp.float32).astype(
        jnp.bfloat16
    )
    enc_queries = enc_queries.reshape(ch_grp, -1, head_dev, HEAD_DIM)
    enc_scores = (
        jnp.einsum("cqhd,ckhd->chqk", enc_queries, cond_key, preferred_element_type=jnp.float32)
        * scale
    )
    enc_weights = plain_softmax(enc_scores)
    enc_att = jnp.einsum(
        "chqk,ckhd->cqhd", enc_weights, cond_value, preferred_element_type=jnp.float32
    ).astype(jnp.bfloat16)
    enc_att = enc_att.reshape(-1, local_width)
    share_rows = enc_att.shape[0] // n_nbr
    summed = lax.psum(jnp.dot(enc_att, enc_out, preferred_element_type=jnp.float32), "nbr")
    encoded_all = normed_rows(ordered, summed, enc_gain)
    encoded_mine = lax.dynamic_slice_in_dim(encoded_all, member * share_rows, share_rows, 0)
    nbr_kv = jnp.dot(
        encoded_all,
        nbr_proj.reshape(enc_width, 2 * local_width),
        preferred_element_type=jnp.float32,
    ).astype(jnp.bfloat16)
    nbr_kv = nbr_kv.reshape(ch_grp, -1, 2 * local_width)
    previous = passed_along(nbr_kv[-1], "seq", 1)
    kv_ext = jnp.concatenate([previous[None], nbr_kv], axis=0)
    key_rows = kv_ext.shape[1]
    kv_ext = kv_ext.reshape(ch_grp + 1, key_rows, 2, head_dev, HEAD_DIM)
    counts_pad = jnp.concatenate([jnp.zeros((1,), jnp.int32), valid_counts], axis=0)
    counts_ext = lax.dynamic_slice_in_dim(counts_pad, seq_index * ch_grp, ch_grp + 1, 0)
    query_pad = jnp.concatenate(
        [
            jnp.zeros((1, local_width), jnp.bfloat16),
            queries,
            jnp.zeros((GROUP - 1, local_width), jnp.bfloat16),
        ],
        axis=0,
    )
    query_pad = query_pad.reshape(ch_grp + 1, GROUP, head_dev, HEAD_DIM)
    local_ids = jnp.arange((ch_grp + 1) * GROUP, dtype=jnp.int32) - 1
    global_ids = seq_index * tok_grp + local_ids
    active = (local_ids >= 0) & (local_ids < tok_grp) & (global_ids % SEQ_LEN >= GROUP - 1)
    active = active.reshape(ch_grp + 1, GROUP)
    key_slot = jnp.arange(key_rows, dtype=jnp.int32) // NLEN
    slot_live = key_slot[None, :] < counts_ext[:, None]
    allowed = active[:, None, :, None] & slot_live[:, None, None, :]
    cca_scores = (
        jnp.einsum(
            "bqhd,bkhd->bhqk", query_pad, kv_ext[:, :, 0], preferred_element_type=jnp.float32
        )
        * scale
    )
    cca_weights = masked_softmax(cca_scores, allowed)
    cca_att = jnp.einsum(
        "bhqk,bkhd->bqhd", cca_weights, kv_ext[:, :, 1], preferred_element_type=jnp.float32
    ).astype(jnp.bfloat16)
    cca_att = cca_att.reshape(-1, local_width)[1 : tok_grp + 1]
    cross_out = lax.psum_scatter(
        jnp.dot(cca_att, out_proj, preferred_element_type=jnp.float32).astype(jnp.bfloat16),
        "nbr",
        scatter_dimension=0,
        tiled=True,
    )
    return (cross_out, encoded_mine)


def solution(mesh):
    return jax.shard_map(
        local,
        mesh=mesh,
        in_specs=(
            P(("seq", "nbr"), None),
            P("seq", "nbr", None),
            P("seq", None),
            P(),
            P(None, None, "nbr"),
            P(None, "nbr"),
            P("nbr", None),
            P(),
            P(None, None, "nbr"),
            P("nbr", None),
        ),
        out_specs=(P(("seq", "nbr"), None), P(("seq", "nbr"), None)),
        check_vma=False,
    )
```

profile of v0, /device:TPU:1, one launch (start us, length us, event | category | flops | bytes accessed | tf_op | source)
XLA Modules:
  0.0 342.4 jit_solution(4652820570967814219)
XLA Ops:
  7.2 0.7 all-gather.3.cloned.1.call-update
  8.0 0.7 all-gather.5.cloned.1.call-update
  8.7 0.7 broadcast_subtract_fusion
  9.4 0.1 copy.31
  9.5 0.1 sub.52
  9.6 0.1 sub.51
  9.6 8.8 %copy.33 = bf16[4096,3,256]{0,2,1:T(8,128)(2,1)} copy(bf16[4096,3,256]{2,0,1:T(8,128)(2,1)} %param.14) | data formatting | bytes 12582912 | tf_op args[4]
  18.5 37.1 %all-gather.3.cloned.1.call-done = bf16[16,128,896]{2,1,0:T(8,128)(2,1)} async-done(((bf16[16,8,896]{2,1,0:T(8,128)(2,1)}), bf16[16,128,896]{2,1,0:T(8,128)(2,1)}) %all-gather.3.cloned.1.call-update) | async-done | bytes 3670032 | tf_op jit(solution)/shard_map/all_gather | solution.py:71
  55.6 4.8 %gather_fusion = bf16[16,128,896]{2,1,0:T(8,128)(2,1)} fusion(bf16[16,128,896]{2,1,0:T(8,128)(2,1)} %all-gather.3.cloned.1.call-done, s32[1024]{0:T(1024)S(1)} %pad_clamp_fusion), kind=kCustom, calls=%fused_computation | custom fusion | bytes 7340096 | tf_op jit(solution)/shard_map/jit(_take)/gather | solution.py:75
  60.4 2.4 bitcast_select_fusion
  62.9 2.3 convolution_convert_fusion.2
  65.1 1.3 reshape.164
  66.5 31.5 %all-gather.5.cloned.1.call-done = bf16[512,4096]{1,0:T(8,128)(2,1)} async-done(((bf16[32,4096]{1,0:T(8,128)(2,1)}), bf16[512,4096]{1,0:T(8,128)(2,1)}) %all-gather.5.cloned.1.call-update) | async-done | bytes 4194320 | tf_op jit(solution)/shard_map/all_gather | solution.py:60
  98.0 7.5 %convolution_convert_fusion.4 = bf16[512,768]{1,0:T(8,128)(2,1)S(1)} fusion(bf16[512,4096]{1,0:T(8,128)(2,1)} %all-gather.5.cloned.1.call-done, bf16[4096,768]{0,1:T(8,128)(2,1)} %bitcast.49), kind=kOutput, calls=%fused_computation.13 | convolution fusion | flops 3221618688 | bytes 11272192 | tf_op jit(solution)/shard_map/dot_general | solution.py:59
  105.5 0.9 fusion.25
  106.5 1.0 reshape.165
  107.5 0.5 convolution_multiply_fusion.1
  108.0 1.0 copy-done.5
  108.9 0.2 fusion.26
  109.2 1.0 reshape.163
  110.2 2.0 fusion.2
  112.3 0.6 copy.37
  112.8 0.3 copy.42
  113.2 0.1 copy-done.9
  113.3 4.3 %fusion.27 = f32[2048,896]{1,0:T(8,128)} fusion(bf16[2048,256]{0,1:T(8,128)(2,1)S(1)} %bitcast.50, bf16[256,896]{1,0:T(8,128)(2,1)S(1)} %copy-done.9), kind=kOutput, calls=%fused_computation.72 | convolution fusion | flops 939524096 | bytes 8847360 | tf_op jit(solution)/shard_map/dot_general | solution.py:90
  117.6 0.2 reduce-scatter.2.cloned.1.call-start
  117.8 0.9 copy-done.7
  118.8 1.1 copy.43
  120.0 0.1 dynamic_slice.6
  120.1 0.1 broadcast_and_fusion
  120.3 126.0 %all-reduce.2.cloned.1.call-done = f32[2048,896]{1,0:T(8,128)} async-done(((f32[2048,896]{1,0:T(8,128)}), f32[2048,896]{1,0:T(8,128)}) %all-reduce.2.cloned.1.call-update) | async-done | bytes 7340048 | tf_op jit(solution)/shard_map/psum | solution.py:90
  246.3 5.5 %multiply_reduce_fusion = f32[2048]{0:T(1024)S(1)} fusion(f32[2048,896]{1,0:T(8,128)} %all-reduce.2.cloned.1.call-done, bf16[16,128,896]{2,1,0:T(8,128)(2,1)} %gather_fusion, pred[2048]{0:T(1024)(128)(4,1)S(1)} %broadcast_bitcast_fusion), kind=kLoop, calls=%fused_computation.3 | loop fusion | flops 9172992 | bytes 11020288 | tf_op jit(solution)/shard_map/reduce_sum | solution.py:35
  251.8 1.9 copy-done.2
  253.7 1.9 multiply_convert_fusion
  255.7 2.4 convolution_convert_fusion.1
  258.1 1.3 copy-done.4
  259.4 3.1 collective-permute-start
  262.5 0.4 and_reduce_fusion
  263.0 0.2 maximum_maximum_fusion
  263.3 4.0 %concatenate.15 = bf16[8,256,2,2,128]{4,3,2,1,0:T(2,128)(2,1)} reshape(bf16[2048,512]{1,0:T(8,128)(2,1)} %copy-done.4) | data formatting | bytes 4194304 | tf_op jit(solution)/shard_map/concatenate | solution.py:100
  267.4 2.3 copy_dynamic-update-slice_fusion
  269.6 0.6 select_reduce_fusion
  270.3 0.5 fusion.6
  270.8 0.5 fusion.4
  271.3 0.3 copy.41
  271.7 3.2 convolution_convert_fusion
  274.9 1.6 constant_dynamic-slice_fusion
  276.6 59.3 %reduce-scatter.2.cloned.1.call-done = bf16[32,4096]{1,0:T(8,128)(2,1)} async-done(((bf16[512,4096]{1,0:T(8,128)(2,1)}), bf16[32,4096]{1,0:T(8,128)(2,1)}) %reduce-scatter.2.cloned.1.call-update) | async-done | bytes 262160 | tf_op jit(solution)/shard_map/reduce_scatter | solution.py:132
  (46 shorter events, 0.8 us)
Async XLA Ops:
  7.2 264.5 %copy-start = (bf16[256,4096]{1,0:T(8,128)(2,1)S(1)}, bf16[256,4096]{1,0:T(8,128)(2,1)}, u32[]{:S(2)}) copy-start(bf16[256,4096]{1,0:T(8,128)(2,1)} %param.19) | copy-start | bytes 6291460
  7.2 48.5 %all-gather.3.cloned.1.call-start = ((), (), s32[]{:S(2)}) async-start(), calls=%async_computation.1 | async-start | bytes 3899392 | tf_op jit(solution)/shard_map/all_gather | solution.py:71
  7.9 90.1 %all-gather.5.cloned.1.call-start = ((), (), s32[]{:S(2)}) async-start(), calls=%async_computation.2 | async-start | bytes 4456448 | tf_op jit(solution)/shard_map/all_gather | solution.py:60
  8.7 237.6 %all-reduce.2.cloned.1.call-start = ((), (), s32[]{:S(2)}) async-start(), calls=%async_computation.3 | async-start | bytes 14680064 | tf_op jit(solution)/shard_map/psum | solution.py:90
  60.4 2.4 copy-start.12
  108.0 1.0 copy-start.5
  112.2 1.0 copy-start.9
  117.6 1.2 copy-start.7
  117.6 2.3 copy-start.11
  117.6 218.2 %reduce-scatter.2.cloned.1.call-start = ((), (), s32[]{:S(2)}) async-start(), calls=%async_computation.4 | async-start | bytes 4456448 | tf_op jit(solution)/shard_map/reduce_scatter | solution.py:132
  120.3 131.5 %copy-start.10 = (f32[896]{0:T(1024)S(1)}, f32[896]{0:T(1024)}, u32[]{:S(2)}) copy-start(f32[896]{0:T(1024)} %param.17) | copy-start | bytes 10756
  246.3 5.5 %copy-start.1 = (bf16[16,128,896]{2,1,0:T(8,128)(2,1)S(1)}, bf16[16,128,896]{2,1,0:T(8,128)(2,1)}, u32[]{:S(2)}) copy-start(bf16[16,128,896]{2,1,0:T(8,128)(2,1)} %gather_fusion) | copy-start | bytes 11010052
  246.3 7.4 %copy-start.2 = (f32[2048,896]{1,0:T(8,128)S(1)}, f32[2048,896]{1,0:T(8,128)}, u32[]{:S(2)}) copy-start(f32[2048,896]{1,0:T(8,128)} %all-reduce.2.cloned.1.call-done) | copy-start | bytes 22020100
  253.7 1.9 copy-start.8
  255.6 2.4 copy-start.3
  255.6 7.3 %copy-start.6 = (bf16[512,256]{1,0:T(8,128)(2,1)S(1)}, bf16[512,256]{1,0:T(8,128)(2,1)}, u32[]{:S(2)}) copy-start(bf16[512,256]{1,0:T(8,128)(2,1)} %get-tuple-element.2) | copy-start | bytes 786436
  258.0 1.3 copy-start.4
  259.4 7.9 %collective-permute-start = (bf16[256,512]{1,0:T(8,128)(2,1)S(1)}, bf16[256,512]{1,0:T(8,128)(2,1)S(1)}, u32[]{:S(2)}, u32[]{:S(2)}) collective-permute-start(bf16[256,512]{1,0:T(8,128)(2,1)S(1)} %slice.34), channel_id=1, source_target_pairs={{0,16},{16,32},{32,48},{48,64},{64,80},{80,96},{96,112},{112,128},... | collective-permute-start | bytes 786440 | tf_op jit(solution)/shard_map/ppermute | solution.py:15
Sparse Core Ops, SparseCore 0:
  9.8 45.7 all-gather.2
  57.5 40.5 all-gather.4
  117.7 128.5 all-reduce.1
  275.0 60.7 reduce-scatter.1
where the time goes:
time: 345 us; the launch traced here: 342 us
  waiting for transfers between devices  255 us (74%)
  local copies, waits for them, and re-layouts  34 us (10%)
  matrix products  23.3 us (7%)
  between operations  14.1 us (4%)
  other arithmetic  12.2 us (4%)
  starting transfers between devices  3.45 us (1%)
    psum x1, waiting for transfers between devices, local(): lax.psum(jnp.dot(enc_att, enc_out, preferred_element_type=jnp.float32), '...  126 us
    reduce_scatter x1, waiting for transfers between devices, local(): lax.psum_scatter(jnp.dot(cca_att, out_proj, preferred_element_type=jnp.fl...  59.3 us
    all_gather x1, waiting for transfers between devices, local(): grp_embed = lax.all_gather(nbr_embed, 'nbr', axis=1, tiled=True)  37.1 us
    all_gather x1, waiting for transfers between devices, local(): lax.all_gather(tokens, 'nbr', axis=0, tiled=True)  31.5 us
    unnamed x31, local copies, waits for them, and re-layouts  15.5 us
    dot_general x1, matrix products, local(): jnp.dot(lax.all_gather(tokens, 'nbr', axis=0, tiled=True), dec_flat, pref...  7.51 us
  transfers between devices with their start and end apart: 5, of which 4 were waited for; matrix products, arithmetic and copies ran while one was open for 8% of the time, Pallas kernels for 0%

commit v1 on v0

v1 whole, which is shorter than its diff:
```python
import jax
import jax.numpy as jnp
from jax import lax
from jax.experimental import pallas as pl
from jax.experimental.pallas import tpu as pltpu
from jax.sharding import PartitionSpec as P

HEAD_DIM = 128
GROUP = 64
NLEN = 128
SEQ_LEN = 2048
CHIPS = 8
F32 = jnp.float32
BF16 = jnp.bfloat16
MESH = pl.DeviceIdType.MESH


def dot(a, b):
    return jnp.dot(a, b, preferred_element_type=F32)


def dot_t(a, b):
    return lax.dot_general(a, b, (((1,), (1,)), ((), ())), preferred_element_type=F32)


def softmax(scores):
    peak = jnp.max(scores, axis=-1, keepdims=True)
    raised = jnp.exp(scores - peak)
    return (raised * (1.0 / jnp.sum(raised, axis=-1, keepdims=True))).astype(BF16)


def wrap(x):
    return lax.rem(x + 2 * CHIPS, CHIPS)


class Place:
    def __init__(self):
        self.seq = lax.axis_index("seq")
        self.n_seq = lax.axis_size("seq")
        me = lax.axis_index("nbr")
        self.me = me
        self.z = me // 2
        self.core = lax.rem(me, 2)
        self.d = 1 - 2 * self.core
        self.sibling = me + self.d

    def on(self, chip):
        return {"nbr": 2 * wrap(chip) + self.core}


class Gather:
    def __init__(self, place, buf, forward_sems, sibling_sems, recv_sems):
        self.p, self.buf = place, buf
        self.fs, self.ss, self.rs = forward_sems, sibling_sems, recv_sems
        self.sent = []

    def copy(self, slot, target, sem):
        return pltpu.make_async_remote_copy(
            src_ref=self.buf.at[slot],
            dst_ref=self.buf.at[slot],
            send_sem=sem,
            recv_sem=self.rs.at[slot],
            device_id=target,
            device_id_type=MESH,
        )

    def start(self, slot, target, sem):
        c = self.copy(slot, target, sem)
        c.start()
        self.sent.append(c)

    def slot(self, chip):
        return 2 * wrap(chip) + self.p.core

    def to_sibling(self, chip, i):
        self.start(self.slot(chip), {"nbr": self.p.sibling}, self.ss.at[i])

    def arrived(self, slot):
        self.copy(slot, {"nbr": self.p.sibling}, self.ss.at[0]).wait_recv()

    def own(self):
        z = self.p.z
        self.start(self.slot(z), self.p.on(z + 1), self.fs.at[0])
        self.start(self.slot(z), self.p.on(z - 1), self.fs.at[1])
        self.to_sibling(z, 0)

    def step(self, h):
        z, d = self.p.z, self.p.d
        if h < 3:
            for j, sign in enumerate((1, -1)):
                self.arrived(self.slot(z - sign * h))
                self.start(self.slot(z - sign * h), self.p.on(z + sign), self.fs.at[2 * h + j])
                self.to_sibling(z - sign * h, 2 * h - 1 + j)
        elif h == 3:
            self.arrived(self.slot(z - 3 * d))
            self.start(self.slot(z - 3 * d), self.p.on(z + d), self.fs.at[6])
            self.to_sibling(z - 3 * d, 5)
            self.arrived(self.slot(z + 3 * d))
            self.to_sibling(z + 3 * d, 6)
        else:
            self.arrived(self.slot(z + 4))
            self.to_sibling(z + 4, 7)

    def from_sibling(self, chip):
        self.arrived(2 * wrap(chip) + 1 - self.p.core)

    def drain(self):
        for c in self.sent:
            c.wait_send()


class Reduce:
    def __init__(self, place, part, from_sib, box, out, sems):
        self.p, self.part, self.from_sib, self.box, self.out = place, part, from_sib, box, out
        self.sib_send, self.sib_recv, self.send, self.recv = sems

    def sign(self, i):
        return jnp.where((i == 0) | (lax.rem(i, 2) == 1), self.p.d, -self.p.d)

    def dest(self, i):
        return wrap(self.p.z + self.sign(i) * (4 - (i + 1) // 2))

    def sib_copy(self, i):
        c = self.dest(i)
        return pltpu.make_async_remote_copy(
            src_ref=self.part.at[c, 1 - self.p.core],
            dst_ref=self.from_sib.at[c],
            send_sem=self.sib_send.at[c],
            recv_sem=self.sib_recv.at[c],
            device_id={"nbr": self.p.sibling},
            device_id_type=MESH,
        )

    def ring_copy(self, i, land):
        return pltpu.make_async_remote_copy(
            src_ref=self.out.at[i],
            dst_ref=self.box.at[land],
            send_sem=self.send.at[i],
            recv_sem=self.recv.at[land],
            device_id=self.p.on(self.p.z + self.sign(i)),
            device_id_type=MESH,
        )

    def chip_sum(self, i):
        c = self.dest(i)
        return self.part[c, self.p.core].astype(F32) + self.from_sib[c].astype(F32)

    def item(self, i):
        self.sib_copy(i).wait_recv()
        starts = (i == 0) | (i == 2)

        @pl.when(starts)
        def _():
            self.out[i] = self.chip_sum(i).astype(BF16)

        @pl.when(jnp.logical_not(starts))
        def _():
            self.ring_copy(i, i).wait_recv()
            self.out[i] = (self.chip_sum(i) + self.box[i].astype(F32)).astype(BF16)

        self.ring_copy(i, jnp.where(i == 0, 1, i + 2)).start()

    def run(self, make):
        def body(i, _):
            make(self.dest(i))
            self.sib_copy(i).start()

            @pl.when(i >= 1)
            def _():
                self.item(i - 1)

            return 0

        lax.fori_loop(0, CHIPS, body, 0)

    def total(self):
        self.sib_copy(7).wait_recv()
        self.ring_copy(0, 7).wait_recv()
        self.ring_copy(0, 8).wait_recv()
        return self.chip_sum(7) + self.box[7].astype(F32) + self.box[8].astype(F32)

    def drain(self):
        def body(i, _):
            self.ring_copy(i, jnp.where(i == 0, 1, i + 2)).wait_send()
            self.sib_copy(i).wait_send()
            return 0

        lax.fori_loop(0, CHIPS - 1, body, 0)
        self.sib_copy(7).wait_send()


def kernel(
    tok_in, nbr_in, table, counts, dec_in, wq_in, wo_in, gain, wkv_in, wout_in,
    out_ref, enc_ref,
    tok_all, nbr_all, nbr_raw, nbr32, wdec, wq, wo, wkv, wout,
    qpad, cond, encq, ppart, psib, pbox, pout, enc_all, att, opart, osib, obox, oout,
    hq, hq_got, ha, ha_got,
    load_sems, tok_f, tok_s, tok_r, nbr_f, nbr_s, nbr_r, enc_f, enc_s, enc_r,
    p0, p1, p2, p3, o0, o1, o2, o3, halo_sems,
):
    p = Place()
    z, core = p.z, p.core
    scale = 1.0 / HEAD_DIM**0.5
    heads = wq.shape[1] // HEAD_DIM
    width = wq.shape[1]

    loads = []
    for j, (src, dst) in enumerate(
        ((tok_in, tok_all.at[p.me]), (nbr_in, nbr_raw), (dec_in, wdec), (wq_in, wq), (wo_in, wo), (wkv_in, wkv), (wout_in, wout))
    ):
        c = pltpu.make_async_copy(src, dst, load_sems.at[j])
        c.start()
        loads.append(c)

    ahead = lax.rem(p.seq + 1, p.n_seq)
    behind = lax.rem(p.seq + p.n_seq - 1, p.n_seq)
    barrier = pltpu.get_barrier_semaphore()
    for who in (p.on(z + 1), p.on(z - 1), {"nbr": p.sibling}, {"seq": ahead}, {"seq": behind}):
        pl.semaphore_signal(barrier, inc=1, device_id=who, device_id_type=MESH)
    loads[1].wait()
    nbr32[...] = nbr_raw[...].astype(F32)
    for c in range(CHIPS):
        pair = [nbr32[lax.rem(table[c, k], nbr32.shape[0])] for k in range(2)]
        nbr_all[p.me, pl.ds(16 * c, 16), :] = jnp.concatenate(pair, axis=0).astype(BF16)
    loads[0].wait()
    pl.semaphore_wait(barrier, 5)

    tok = Gather(p, tok_all, tok_f, tok_s, tok_r)
    nbr = Gather(p, nbr_all, nbr_f, nbr_s, nbr_r)
    tok.own()
    tok.step(1)
    nbr.own()
    tok.step(2)
    nbr.step(1)
    tok.step(3)
    nbr.step(2)
    tok.step(4)
    for h in range(CHIPS):
        tok.from_sibling(z + h)
    loads[2].wait()

    def project(j):
        x = tok_all[...].reshape(16 * tok_all.shape[1], tok_all.shape[2])
        return dot(x, wdec[j])

    cond[0] = project(1).astype(BF16)
    nbr.step(3)
    cond[1] = project(2).astype(BF16)
    loads[3].wait()

    def enc_queries(chip):
        for k in range(2):
            n = 2 * wrap(chip) + k
            encq[n] = dot(nbr_all[n], wq[...]).astype(BF16)

    for h in (0, 1, -1, 2, -2):
        nbr.from_sibling(z + h)

    def early(i, _):
        enc_queries(z + i - 2)
        return 0

    lax.fori_loop(0, 5, early, 0)
    nbr.step(4)
    qpad[pl.ds(1, 512), :] = project(0).astype(BF16).astype(F32)
    hq[...] = qpad[pl.ds(0, GROUP), :].astype(BF16)

    def halo(src, dst, target, j):
        return pltpu.make_async_remote_copy(
            src_ref=src, dst_ref=dst, send_sem=halo_sems.at[2 * j], recv_sem=halo_sems.at[2 * j + 1],
            device_id={"seq": target}, device_id_type=MESH,
        )

    send_q = halo(hq, hq_got, behind, 0)
    send_q.start()
    for h in (3, -3, 4):
        nbr.from_sibling(z + h)

    def late(i, _):
        enc_queries(z + i + 3)
        return 0

    lax.fori_loop(0, 3, late, 0)
    loads[4].wait()

    def encode(c):
        queries = encq[:, pl.ds(pl.multiple_of(16 * c, 16), 16), :].reshape(2 * NLEN, width)
        mine = pl.ds(pl.multiple_of(GROUP * c, GROUP), GROUP)
        per_head = []
        for h in range(heads):
            cols = slice(HEAD_DIM * h, HEAD_DIM * (h + 1))
            weights = softmax(dot_t(queries[:, cols], cond[0, mine, cols]) * scale)
            per_head.append(dot(weights, cond[1, mine, cols]).astype(BF16))
        summed = dot(jnp.concatenate(per_head, axis=1), wo[...])
        summed = summed.reshape(16, 2, 8, summed.shape[1])
        for k in range(2):
            ppart[c, k] = summed[:, k].reshape(NLEN, summed.shape[3]).astype(BF16)

    enc_sum = Reduce(p, ppart, psib, pbox, pout, (p0, p1, p2, p3))
    enc_sum.run(encode)
    raw = nbr_all[:, pl.ds(pl.multiple_of(16 * z, 16), 16), :].astype(F32).reshape(16, 2, 8, -1)
    raw = jnp.where(core == 0, raw[:, 0], raw[:, 1]).reshape(NLEN, -1)
    combined = raw + enc_sum.total()
    factor = lax.rsqrt(jnp.mean(combined * combined, axis=-1, keepdims=True) + 1e-06)
    encoded = (combined * factor * gain[...]).astype(BF16)
    enc_all[p.me] = encoded
    enc = Gather(p, enc_all, enc_f, enc_s, enc_r)
    enc.own()
    enc_ref[...] = encoded
    loads[5].wait()
    loads[6].wait()
    send_q.wait_recv()

    def attend(g, last):
        rows = enc_all[pl.ds(2 * g, 2)].reshape(2 * NLEN, -1)
        keys = dot(rows, wkv[0]).astype(BF16)
        values = dot(rows, wkv[1]).astype(BF16)
        queries = qpad[pl.ds(pl.multiple_of(GROUP * (g + 1), GROUP), GROUP), :]
        first = lax.broadcasted_iota(jnp.int32, queries.shape, 0) == 0
        queries = jnp.where(first | jnp.logical_not(last), queries, hq_got[...].astype(F32)).astype(BF16)
        count = counts[p.seq * CHIPS + g]
        live = lax.broadcasted_iota(jnp.int32, (GROUP, 2 * NLEN), 1) < NLEN * count
        per_head = []
        for h in range(heads):
            cols = slice(HEAD_DIM * h, HEAD_DIM * (h + 1))
            scores = jnp.where(live, dot_t(queries[:, cols], keys[:, cols]) * scale, -1e30)
            per_head.append(dot(softmax(scores), values[:, cols]))
        got = jnp.concatenate(per_head, axis=1).astype(BF16)
        att[pl.ds(pl.multiple_of(GROUP * (g + 1), GROUP), GROUP), :] = got.astype(F32)

    def attend_all(first, count):
        def body(i, _):
            sign = jnp.where(lax.rem(i, 2) == 1, 1, -1)
            g = wrap(z + sign * ((i + 1) // 2))
            attend(g, g == CHIPS - 1)
            return 0

        lax.fori_loop(first, first + count, body, 0)

    enc.step(1)
    enc.from_sibling(z)
    attend_all(0, 1)
    enc.step(2)
    enc.from_sibling(z + 1)
    enc.from_sibling(z - 1)
    attend_all(1, 2)
    enc.step(3)
    enc.from_sibling(z + 2)
    enc.from_sibling(z - 2)
    attend_all(3, 2)
    enc.step(4)
    enc.from_sibling(z + 3)
    enc.from_sibling(z - 3)
    attend_all(5, 2)
    enc.from_sibling(z + 4)
    attend_all(7, 1)
    ha[...] = att[pl.ds(GROUP * CHIPS, GROUP), :].astype(BF16)
    send_a = halo(ha, ha_got, ahead, 1)
    send_a.start()
    send_a.wait_recv()
    begins = lax.rem(p.seq * (GROUP * CHIPS), SEQ_LEN) == 0
    att[pl.ds(0, GROUP), :] = jnp.where(begins, 0.0, ha_got[...].astype(F32))

    half = GROUP // 2
    block = 512

    def project_out(c):
        wide = att[pl.ds(pl.multiple_of(GROUP * c, GROUP), GROUP + 8), :]
        rows = wide[1 : GROUP + 1].astype(BF16)

        def body(j, _):
            cols = pl.ds(pl.multiple_of(j * block, block), block)
            y = dot(rows, wout[:, cols]).astype(BF16)
            opart[c, 0, :, cols] = y[:half]
            opart[c, 1, :, cols] = y[half:]
            return 0

        lax.fori_loop(0, wout.shape[1] // block, body, 0)

    out_sum = Reduce(p, opart, osib, obox, oout, (o0, o1, o2, o3))
    out_sum.run(project_out)
    out_ref[...] = out_sum.total().astype(BF16)

    for g in (tok, nbr, enc):
        g.drain()
    enc_sum.drain()
    out_sum.drain()
    send_q.wait_send()
    send_a.wait_send()


def local(
    tokens, nbr_embed, neighbour_table, valid_counts, dec_proj, enc_query, enc_out, enc_gain, nbr_proj, out_proj
):
    rows, model = tokens.shape
    nbrs, piece, enc_width = nbr_embed.shape
    width = enc_query.shape[1]
    chunk = nbrs * piece
    dma = pltpu.SemaphoreType.DMA
    scratch = [
        pltpu.VMEM((16, rows, model), BF16),
        pltpu.VMEM((16, chunk, enc_width), BF16),
        pltpu.VMEM((nbrs, piece, enc_width), BF16),
        pltpu.VMEM((nbrs, piece, enc_width), F32),
        pltpu.VMEM((3, model, width), BF16),
        pltpu.VMEM((enc_width, width), BF16),
        pltpu.VMEM((width, enc_width), BF16),
        pltpu.VMEM((2, enc_width, width), BF16),
        pltpu.VMEM((width, model), BF16),
        pltpu.VMEM((GROUP * (CHIPS + 1) + 8, width), F32),
        pltpu.VMEM((2, GROUP * CHIPS, width), BF16),
        pltpu.VMEM((16, chunk, width), BF16),
        pltpu.VMEM((CHIPS, 2, NLEN, enc_width), BF16),
        pltpu.VMEM((CHIPS, NLEN, enc_width), BF16),
        pltpu.VMEM((CHIPS + 1, NLEN, enc_width), BF16),
        pltpu.VMEM((CHIPS - 1, NLEN, enc_width), BF16),
        pltpu.VMEM((16, NLEN, enc_width), BF16),
        pltpu.VMEM((GROUP * (CHIPS + 1) + 8, width), F32),
        pltpu.VMEM((CHIPS, 2, rows, model), BF16),
        pltpu.VMEM((CHIPS, rows, model), BF16),
        pltpu.VMEM((CHIPS + 1, rows, model), BF16),
        pltpu.VMEM((CHIPS - 1, rows, model), BF16),
        *[pltpu.VMEM((GROUP, width), BF16)] * 4,
        dma((7,)),
        *[dma((7,)), dma((8,)), dma((16,))] * 3,
        *[dma((8,)), dma((8,)), dma((7,)), dma((9,))] * 2,
        dma((4,)),
    ]
    any_space = pl.BlockSpec(memory_space=pl.ANY)
    smem = pl.BlockSpec(memory_space=pltpu.SMEM)
    vmem = pl.BlockSpec(memory_space=pltpu.VMEM)
    return pl.pallas_call(
        kernel,
        out_shape=(
            jax.ShapeDtypeStruct((rows, model), BF16),
            jax.ShapeDtypeStruct((NLEN, enc_width), BF16),
        ),
        in_specs=[any_space, any_space, smem, smem, any_space, any_space, any_space, vmem, any_space, any_space],
        out_specs=(vmem, vmem),
        scratch_shapes=scratch,
        compiler_params=pltpu.CompilerParams(
            collective_id=0, has_side_effects=True, vmem_limit_bytes=60 * 2**20
        ),
        name="retrieval",
    )(
        tokens,
        nbr_embed,
        neighbour_table,
        valid_counts,
        jnp.transpose(dec_proj, (1, 0, 2)),
        enc_query,
        enc_out,
        enc_gain.reshape(1, enc_width),
        jnp.transpose(nbr_proj, (1, 0, 2)),
        out_proj,
    )


def solution(mesh):
    return jax.shard_map(
        local,
        mesh=mesh,
        in_specs=(
            P(("seq", "nbr"), None),
            P("seq", "nbr", None),
            P("seq", None),
            P(),
            P(None, None, "nbr"),
            P(None, "nbr"),
            P("nbr", None),
            P(),
            P(None, None, "nbr"),
            P("nbr", None),
        ),
        out_specs=(P(("seq", "nbr"), None), P(("seq", "nbr"), None)),
        check_vma=False,
    )
```

time: 345 us -> 160 us (0.46)
  waiting for transfers between devices: 255 us -> 0 us
  Pallas kernels: 0 us -> 151 us
  local copies, waits for them, and re-layouts: 34 us -> 8.16 us
  matrix products: 23.3 us -> 0 us
  between operations: 14.1 us -> 0.64 us
  other arithmetic: 12.2 us -> 0 us
  starting transfers between devices: 3.45 us -> 0 us
    pallas_call x0 -> x1, Pallas kernels: none -> 151 us  [local(): pl.pallas_call(kernel, out_shape=(jax.ShapeDtypeStruct((rows, model), BF1...]
    psum x1 -> x0, waiting for transfers between devices: 126 us -> none  [local(): lax.psum(jnp.dot(enc_att, enc_out, preferred_element_type=jnp.float32), '...]
    all_gather x2 -> x0, waiting for transfers between devices: 68.6 us -> none  [the longest x1 37.1 us: local(): grp_embed = lax.all_gather(nbr_embed, 'nbr', axis=1, tiled=True)]
    reduce_scatter x1 -> x0, waiting for transfers between devices: 59.3 us -> none  [local(): lax.psum_scatter(jnp.dot(cca_att, out_proj, preferred_element_type=jnp.fl...]
    dot_general x9 -> x0, matrix products: 23.3 us -> none  [the longest x1 7.51 us: local(): jnp.dot(lax.all_gather(tokens, 'nbr', axis=0, tiled=True), dec_flat, pref...]
    unnamed x31 -> x4, local copies, waits for them, and re-layouts: 15.5 us -> 6.89 us
    concatenate x5 -> x0, local copies, waits for them, and re-layouts: 6.36 us -> none  [the longest x3 6.28 us: local(): kv_ext = jnp.concatenate([previous[None], nbr_kv], axis=0)]
    reduce_sum x2 -> x0, other arithmetic: 5.97 us -> none  [the longest x1 5.5 us: normed_rows(): jnp.mean(combined * combined, axis=-1, keepdims=True) + 1e-06]
  transfers between devices with their start and end apart: 5 -> 0, of which waited for: 4 -> 0; matrix products, arithmetic and copies ran while one was open for 8% -> 0% of each run, Pallas kernels for 0% -> 0%
where the time goes in v1:
time: 160 us; the launch traced here: 159 us
  Pallas kernels  151 us (94%)
  local copies, waits for them, and re-layouts  8.16 us (5%)
    pallas_call x1, Pallas kernels, local(): pl.pallas_call(kernel, out_shape=(jax.ShapeDtypeStruct((rows, model), BF1...  151 us
    unnamed x4, local copies, waits for them, and re-layouts  6.89 us

profile of v1, /device:TPU:1, one launch (start us, length us, event | category | flops | bytes accessed | tf_op | source)
XLA Modules:
  0.0 159.3 jit_solution(16209038579950364967)
XLA Ops:
  0.6 1.3 reshape.7.gain
  1.9 1.3 copy.13.table
  3.2 2.2 %copy.15 = bf16[896,2,256]{2,0,1:T(8,128)(2,1)} copy(bf16[896,2,256]{2,1,0:T(2,128)(2,1)} %param.18) | data formatting | bytes 1835008 | tf_op args[8]
  5.5 150.5 %retrieval.1 = (bf16[32,4096]{1,0:T(8,128)(2,1)}, bf16[128,896]{1,0:T(8,128)(2,1)}) custom-call(bf16[32,4096]{1,0:T(8,128)(2,1)} %tok_in.1, bf16[16,8,896]{2,1,0:T(8,128)(2,1)} %nbr_in.1, s32[8,2]{1,0:T(8,128)} %copy.13.table, s32[128]{0:T(128)} %counts.1, bf16[3,4096,256]{2,1,0:T(8,128)(2,1)} %bitcast.4, bf16[896,256]{1,0:T(8,128)(2,1)} %wq_in.1, ...), custom_call_target="tpu_custom_call" | custom-call | tf_op jit(solution)/shard_map/retrieval/pallas_call | solution.py:432
  156.0 1.7 %copy.18 = bf16[32,4096]{1,0:T(8,128)(2,1)} copy(bf16[32,4096]{1,0:T(8,128)(2,1)} %get-tuple-element.4) | data formatting | bytes 524288
  157.7 1.6 %copy.19 = bf16[128,896]{1,0:T(8,128)(2,1)} copy(bf16[128,896]{1,0:T(8,128)(2,1)} %get-tuple-element.5) | data formatting | bytes 458752

commit v2 on v0

v2 whole, which is shorter than its diff:
```python
import functools
import types

import jax
import jax.numpy as jnp
from jax import lax
from jax.experimental import pallas as pl
from jax.experimental.pallas import tpu as pltpu
from jax.sharding import PartitionSpec as P

HEAD_DIM = 128
GROUP = 64
NLEN = 128
SEQ_LEN = 2048
CHIPS = 8
F32 = jnp.float32
BF16 = jnp.bfloat16
MESH = pl.DeviceIdType.MESH


def dot(a, b):
    return jnp.dot(a, b, preferred_element_type=F32)


def dot_t(a, b):
    return lax.dot_general(a, b, (((1,), (1,)), ((), ())), preferred_element_type=F32)


def softmax(scores):
    peak = jnp.max(scores, axis=-1, keepdims=True)
    raised = jnp.exp(scores - peak)
    return (raised * (1.0 / jnp.sum(raised, axis=-1, keepdims=True))).astype(BF16)


def wrap(x):
    return lax.rem(x + 2 * CHIPS, CHIPS)


class Place:
    def __init__(self):
        self.seq = lax.axis_index("seq")
        self.n_seq = lax.axis_size("seq")
        me = lax.axis_index("nbr")
        self.me = me
        self.z = me // 2
        self.core = lax.rem(me, 2)
        self.d = 1 - 2 * self.core
        self.sibling = me + self.d

    def on(self, chip):
        return {"nbr": 2 * wrap(chip) + self.core}

    def nth(self, i):
        sign = jnp.where(lax.rem(i, 2) == 1, 1, -1)
        return wrap(self.z + sign * ((i + 1) // 2))


class Gather:
    def __init__(self, place, ref, forward_sems, recv_sems, sibling_sems=None):
        self.p, self.ref = place, ref
        self.fs, self.rs, self.ss = forward_sems, recv_sems, sibling_sems
        self.sent = []

    def copy(self, chip, core, target, sem):
        slot = 2 * wrap(chip) + core
        return pltpu.make_async_remote_copy(
            src_ref=self.ref(slot),
            dst_ref=self.ref(slot),
            send_sem=sem,
            recv_sem=self.rs.at[slot],
            device_id=target,
            device_id_type=MESH,
        )

    def start(self, chip, target, sem):
        c = self.copy(chip, self.p.core, target, sem)
        c.start()
        self.sent.append(c)

    def to_sibling(self, chip, i):
        if self.ss is not None:
            self.start(chip, {"nbr": self.p.sibling}, self.ss.at[i])

    def arrived(self, chip):
        self.copy(chip, self.p.core, {"nbr": self.p.sibling}, self.fs.at[0]).wait_recv()

    def from_sibling(self, chip):
        self.copy(chip, 1 - self.p.core, {"nbr": self.p.sibling}, self.fs.at[0]).wait_recv()

    def own(self):
        z = self.p.z
        self.start(z, self.p.on(z + 1), self.fs.at[0])
        self.start(z, self.p.on(z - 1), self.fs.at[1])
        self.to_sibling(z, 0)

    def step(self, h):
        z, d = self.p.z, self.p.d
        if h < 3:
            for j, sign in enumerate((1, -1)):
                self.arrived(z - sign * h)
                self.start(z - sign * h, self.p.on(z + sign), self.fs.at[2 * h + j])
                self.to_sibling(z - sign * h, 2 * h - 1 + j)
        elif h == 3:
            self.arrived(z - 3 * d)
            self.start(z - 3 * d, self.p.on(z + d), self.fs.at[6])
            self.to_sibling(z - 3 * d, 5)
            self.arrived(z + 3 * d)
            self.to_sibling(z + 3 * d, 6)
        else:
            self.arrived(z + 4)
            self.to_sibling(z + 4, 7)

    def drain(self):
        for c in self.sent:
            c.wait_send()


class Spread:
    def __init__(self, place, piece, slab, first, second, sems):
        self.p, self.piece, self.slab = place, piece, slab
        (self.a, self.to_first), (self.b, self.to_second) = first, second
        self.bs, self.br, self.cs, self.cr, self.ds, self.dr, self.es, self.er = sems
        self.sent = []

    def copy(self, ref, target, send, recv):
        return pltpu.make_async_remote_copy(
            src_ref=ref, dst_ref=ref, send_sem=send, recv_sem=recv, device_id=target, device_id_type=MESH
        )

    def start(self, *copy):
        c = self.copy(*copy)
        c.start()
        self.sent.append(c)

    def send_both(self, i, ref, to, send, recv):
        for j, sign in enumerate((1, -1)):
            self.start(ref, to(sign), send.at[i, j], recv.at[i, j])

    def pass_on(self, i, ref, to, arrived, send, recv):
        for j, sign in enumerate((1, -1)):
            self.copy(ref(-sign), to(sign), send.at[i], arrived.at[i, j]).wait_recv()
        sign = 1 if i % 2 else -1
        self.start(ref(-sign), to(sign), send.at[i], recv.at[i])

    def piece_at(self, i, shift):
        return self.piece(self.p.nth(i), lax.rem(self.a + shift + 4, 4))

    def slab_at(self, i, shift):
        return self.slab(self.p.nth(i), lax.rem(self.b + shift + 4, 4))

    def pieces_out(self, i):
        self.send_both(i, self.piece_at(i, 0), self.to_first, self.bs, self.br)

    def pieces_on(self, i):
        self.pass_on(i, functools.partial(self.piece_at, i), self.to_first, self.br, self.cs, self.cr)

    def slabs_out(self, i):
        self.copy(self.piece_at(i, 2), self.to_first(1), self.cs.at[i], self.cr.at[i]).wait_recv()
        self.send_both(i, self.slab_at(i, 0), self.to_second, self.ds, self.dr)

    def slabs_on(self, i):
        self.pass_on(i, functools.partial(self.slab_at, i), self.to_second, self.dr, self.es, self.er)

    def ready(self, i):
        self.copy(self.slab_at(i, 2), self.to_second(1), self.es.at[i], self.er.at[i]).wait_recv()

    def drain(self):
        for c in self.sent:
            c.wait_send()


class Reduce:
    def __init__(self, place, part, from_sib, box, out, sems):
        self.p, self.part, self.from_sib, self.box, self.out = place, part, from_sib, box, out
        self.sib_send, self.sib_recv, self.send, self.recv = sems

    def sign(self, i):
        return jnp.where((i == 0) | (lax.rem(i, 2) == 1), self.p.d, -self.p.d)

    def dest(self, i):
        return wrap(self.p.z + self.sign(i) * (4 - (i + 1) // 2))

    def sib_copy(self, k, c):
        return pltpu.make_async_remote_copy(
            src_ref=self.part.at[k, c, 1 - self.p.core],
            dst_ref=self.from_sib.at[k, c],
            send_sem=self.sib_send.at[k, c],
            recv_sem=self.sib_recv.at[k, c],
            device_id={"nbr": self.p.sibling},
            device_id_type=MESH,
        )

    def ring_copy(self, k, i, land):
        return pltpu.make_async_remote_copy(
            src_ref=self.out.at[k, i],
            dst_ref=self.box.at[k, land],
            send_sem=self.send.at[k, i],
            recv_sem=self.recv.at[k, land],
            device_id=self.p.on(self.p.z + self.sign(i)),
            device_id_type=MESH,
        )

    def chip_sum(self, k, i):
        c = self.dest(i)
        return self.part[k, c, self.p.core].astype(F32) + self.from_sib[k, c].astype(F32)

    def item(self, k, i):
        self.sib_copy(k, self.dest(i)).wait_recv()
        starts = (i == 0) | (i == 2)

        @pl.when(starts)
        def _():
            self.out[k, i] = self.chip_sum(k, i).astype(BF16)

        @pl.when(jnp.logical_not(starts))
        def _():
            self.ring_copy(k, i, i).wait_recv()
            self.out[k, i] = (self.chip_sum(k, i) + self.box[k, i].astype(F32)).astype(BF16)

        self.ring_copy(k, i, jnp.where(i == 0, 1, i + 2)).start()

    def total(self, k):
        self.sib_copy(k, self.p.z).wait_recv()
        self.ring_copy(k, 0, 7).wait_recv()
        self.ring_copy(k, 0, 8).wait_recv()
        return self.chip_sum(k, jnp.int32(7)) + self.box[k, 7].astype(F32) + self.box[k, 8].astype(F32)

    def drain(self):
        def body(i, _):
            for k in range(2):
                self.ring_copy(k, i, i).wait_send()
                self.sib_copy(k, i).wait_send()
            return 0

        lax.fori_loop(0, CHIPS - 1, body, 0)
        for k in range(2):
            self.sib_copy(k, CHIPS - 1).wait_send()


def kernel(names, *refs):
    r = types.SimpleNamespace(**dict(zip(names, refs, strict=True)))
    p = Place()
    z, core = p.z, p.core
    scale = 1.0 / HEAD_DIM**0.5
    width = r.wkv.shape[2]
    heads = width // HEAD_DIM
    model = r.wout.shape[1]
    enc_width = r.wkv.shape[1]
    half_model = model // 2
    half_rows = NLEN // 2
    x, y = p.seq // 4, lax.rem(p.seq, 4)

    loads = []
    for j, (src, dst) in enumerate(
        (
            (r.nbr_in, r.nbr_raw),
            (r.wq_in, r.wq_all.at[z]),
            (r.wo_in, r.wo_all.at[z]),
            (r.tok_in.at[:, pl.ds(0, half_model)], r.tok_all.at[0, p.me]),
            (r.tok_in.at[:, pl.ds(half_model, half_model)], r.tok_all.at[1, p.me]),
            (r.dec_in, r.wdec),
            (r.wkv_in, r.wkv_raw),
            (r.wout_in, r.wout),
        )
    ):
        c = pltpu.make_async_copy(src, dst, r.load_sems.at[j])
        c.start()
        loads.append(c)
    load_nbr, load_q, load_o, load_tok0, load_tok1, load_dec, load_kv, load_out = loads

    def to_x(shift):
        return {"seq": 4 * lax.rem(x + shift + 4, 4) + y}

    def to_y(shift):
        return {"seq": 4 * x + lax.rem(y + shift + 4, 4)}

    ahead = lax.rem(p.seq + 1, p.n_seq)
    behind = lax.rem(p.seq + p.n_seq - 1, p.n_seq)
    partners = [p.on(z + h) for h in range(1, CHIPS)]
    partners += [{"nbr": p.sibling}, to_x(1), to_x(-1), to_y(1), to_y(-1), {"seq": ahead}, {"seq": behind}]
    barrier = pltpu.get_barrier_semaphore()
    for who in partners:
        pl.semaphore_signal(barrier, inc=1, device_id=who, device_id_type=MESH)
    load_nbr.wait()
    r.nbr32[...] = r.nbr_raw[...].astype(F32)
    for c in range(CHIPS):
        pair = [r.nbr32[lax.rem(r.table[k, c], r.nbr32.shape[0])] for k in range(2)]
        r.nbr_send[c] = jnp.concatenate(pair, axis=0).astype(BF16)
    r.nbr_all[z, core] = r.nbr_send[z]
    for c in (load_q, load_o, load_tok0, load_tok1):
        c.wait()
    pl.semaphore_wait(barrier, len(partners))

    def query_piece(chip, a):
        rows = pl.ds(pl.multiple_of(224 * y + 112 * (a // 2), 16), 112)
        return r.wq_all.at[chip, rows, pl.ds(pl.multiple_of(128 * lax.rem(a, 2), 128), 128)]

    def query_slab(chip, b):
        return r.wq_all.at[chip, pl.ds(pl.multiple_of(224 * b, 16), 224)]

    def out_piece(chip, a):
        return r.wo_all.at[chip, pl.ds(pl.multiple_of(64 * x + 16 * a, 16), 16)]

    def out_slab(chip, b):
        return r.wo_all.at[chip, pl.ds(pl.multiple_of(64 * b, 16), 64)]

    def stream(name, k, ref, sibling=True):
        sems = [getattr(r, name + end).at[k] for end in ("_f", "_r", "_s")[: 2 + sibling]]
        return Gather(p, ref, *sems)

    tok, enc = ([stream(name, k, getattr(r, name + "_all").at[k].at.__getitem__) for k in range(2)] for name in ("tok", "enc"))
    weights_z = [
        stream("wz", 0, lambda slot: query_piece(slot // 2, x), False),
        stream("wz", 1, lambda slot: out_piece(slot // 2, y), False),
    ]
    spread_sems = [getattr(r, "x" + c) for c in "abcdefgh"]
    weights_xy = [
        Spread(p, query_piece, query_slab, (x, to_x), (y, to_y), [s.at[0] for s in spread_sems]),
        Spread(p, out_piece, out_slab, (y, to_y), (x, to_x), [s.at[1] for s in spread_sems]),
    ]

    def weights(what, *items):
        for i in items:
            for w in weights_xy:
                getattr(w, what)(i)

    def weights_step(h):
        for w in weights_z:
            w.step(h)

    def remote(src, dst, target, send, recv):
        return pltpu.make_async_remote_copy(
            src_ref=src, dst_ref=dst, send_sem=send, recv_sem=recv, device_id=target, device_id_type=MESH
        )

    def halo(src, dst, target, j):
        return remote(src, dst, {"seq": target}, r.halo_sems.at[2 * j], r.halo_sems.at[2 * j + 1])

    send_q = halo(r.hq, r.hq_got, behind, 0)
    send_a = halo(r.ha, r.ha_got, ahead, 1)

    def nbr_copy(h):
        return remote(
            r.nbr_send.at[wrap(z + h)], r.nbr_all.at[z, core], p.on(z + h), r.nbr_sems.at[0, h], r.nbr_sems.at[1, z]
        )

    def nbr_arrived(h):
        chip = wrap(z + h)
        remote(
            r.nbr_send.at[0], r.nbr_all.at[chip, core], p.on(chip), r.nbr_sems.at[0, 0], r.nbr_sems.at[1, chip]
        ).wait_recv()

    nbr_sib = remote(
        r.nbr_all.at[:, core], r.nbr_all.at[:, core], {"nbr": p.sibling}, r.pair_sems.at[0], r.pair_sems.at[1]
    )
    nbr_sib_in = remote(
        r.nbr_all.at[:, 1 - core], r.nbr_all.at[:, 1 - core], {"nbr": p.sibling}, r.pair_sems.at[0], r.pair_sems.at[1]
    )

    def cond_copy(j, h):
        mine = pl.ds(pl.multiple_of(GROUP * wrap(z + h), GROUP), GROUP)
        return remote(
            r.cond.at[j, mine], r.cond_got.at[z, j], p.on(z + h), r.cond_s.at[j, h], r.cond_r.at[j, z]
        )

    def cond_arrived(j, chip):
        remote(
            r.cond.at[j, pl.ds(0, GROUP)], r.cond_got.at[chip, j], p.on(chip), r.cond_s.at[j, 0], r.cond_r.at[j, chip]
        ).wait_recv()

    order = (1, -1, 2, -2, 3, -3, 4)

    def project(j):
        x0, x1 = (r.tok_all[k].reshape(CHIPS * GROUP, half_model) for k in range(2))
        return dot(x0, r.wdec[j, pl.ds(0, half_model)]) + dot(x1, r.wdec[j, pl.ds(half_model, half_model)])

    def make_cond(j):
        r.cond[j] = project(1 + j).astype(BF16)
        for h in order:
            cond_copy(j, h % CHIPS).start()
        r.cond_got[z, j] = r.cond[j, pl.ds(pl.multiple_of(GROUP * z, GROUP), GROUP)]

    def encode(i, _):
        chip = p.nth(i)

        @pl.when(i >= 1)
        def _():
            for j in range(2):
                cond_arrived(j, chip)
            for w in weights_xy:
                w.ready(i)

        queries = dot(r.nbr_all[...].reshape(2 * NLEN, enc_width), r.wq_all[chip]).astype(BF16)
        per_head = []
        for h in range(heads):
            cols = slice(HEAD_DIM * h, HEAD_DIM * (h + 1))
            shares = softmax(dot_t(queries[:, cols], r.cond_got[chip, 0, :, cols]) * scale)
            per_head.append(dot(shares, r.cond_got[chip, 1, :, cols]).astype(BF16))
        term = dot(jnp.concatenate(per_head, axis=1), r.wo_all[chip])

        @pl.when(i == 0)
        def _():
            r.enc_sum[...] = term

        @pl.when(i >= 1)
        def _():
            r.enc_sum[...] += term

        return 0

    def of_slot(rows, slot):
        rows = rows.reshape(16, 2, 8, enc_width)
        return jnp.where(slot == 0, rows[:, 0], rows[:, 1]).reshape(NLEN, enc_width)

    sum_copy = remote(r.sum_out, r.sum_got, {"nbr": p.sibling}, r.pair_sems.at[2], r.pair_sems.at[3])

    def split_kv():
        step = 128

        def body(i, _):
            mine = pl.ds(pl.multiple_of(i * step, step), step)
            both = r.wkv_raw[mine].astype(F32)
            r.wkv[0, mine] = both[:, 0].astype(BF16)
            r.wkv[1, mine] = both[:, 1].astype(BF16)
            return 0

        lax.fori_loop(0, enc_width // step, body, 0)

    def make_kv(k, g):
        rows = r.enc_all[k, pl.ds(2 * g, 2)].reshape(NLEN, enc_width)
        for j in range(2):
            r.kv[j, g, pl.ds(NLEN * k, NLEN)] = dot(rows, r.wkv[j]).astype(BF16)

    def attend(g):
        queries = r.qpad[pl.ds(pl.multiple_of(GROUP * (g + 1), GROUP), GROUP), :]
        own = (lax.broadcasted_iota(jnp.int32, queries.shape, 0) == 0) | (g != CHIPS - 1)
        queries = jnp.where(own, queries, r.hq_got[...].astype(F32)).astype(BF16)
        count = r.counts[p.seq * CHIPS + g]
        key = lax.broadcasted_iota(jnp.int32, (GROUP, 2 * NLEN), 1)
        live = lax.rem(key // half_rows, 2) < count
        per_head = []
        for h in range(heads):
            cols = slice(HEAD_DIM * h, HEAD_DIM * (h + 1))
            scores = jnp.where(live, dot_t(queries[:, cols], r.kv[0, g, :, cols]) * scale, -1e30)
            per_head.append(dot(softmax(scores), r.kv[1, g, :, cols]))
        got = jnp.concatenate(per_head, axis=1).astype(BF16)
        r.att[pl.ds(pl.multiple_of(GROUP * (g + 1), GROUP), GROUP), :] = got.astype(F32)

        @pl.when(g == CHIPS - 1)
        def _():
            r.ha[...] = got
            send_a.start()

    def attend_all(first, count):
        def body(i, _):
            make_kv(1, p.nth(i))
            attend(p.nth(i))
            return 0

        lax.fori_loop(first, first + count, body, 0)

    out_sum = Reduce(p, r.opart, r.osib, r.obox, r.oout, (r.o0, r.o1, r.o2, r.o3))
    half = GROUP // 2
    block = 512

    def make_out(c):
        @pl.when(c == 0)
        def _():
            send_a.wait_recv()
            begins = lax.rem(p.seq * (GROUP * CHIPS), SEQ_LEN) == 0
            r.att[pl.ds(0, GROUP), :] = jnp.where(begins, 0.0, r.ha_got[...].astype(F32))

        wide = r.att[pl.ds(pl.multiple_of(GROUP * c, GROUP), GROUP + 8), :]
        rows = wide[1 : GROUP + 1].astype(BF16)

        for k in range(2):

            def body(j, _, k=k):
                cols = pl.ds(pl.multiple_of(j * block, block), block)
                weight = r.wout[:, pl.ds(pl.multiple_of(k * half_model + j * block, block), block)]
                y = dot(rows, weight).astype(BF16)
                r.opart[k, c, 0, :, cols] = y[:half]
                r.opart[k, c, 1, :, cols] = y[half:]
                return 0

            lax.fori_loop(0, half_model // block, body, 0)
            out_sum.sib_copy(k, c).start()

    def make_outs(chips):
        for c in chips:
            make_out(wrap(c))

    for g in (*weights_z, *tok):
        g.own()
    load_kv.wait()
    split_kv()
    weights_step(1)
    weights("pieces_out", 1, 2)
    tok[0].step(1)
    weights("pieces_on", 1, 2)
    tok[1].step(1)
    weights_step(2)
    weights("slabs_out", 1, 2)
    weights("pieces_out", 3, 4)
    tok[0].step(2)
    weights("pieces_on", 3, 4)
    weights("slabs_on", 1)
    tok[1].step(2)
    weights_step(3)
    weights("slabs_on", 2)
    weights("slabs_out", 3, 4)
    weights("pieces_out", 5, 6)
    tok[0].step(3)
    weights("pieces_on", 5, 6)
    weights("slabs_on", 3)
    tok[1].step(3)
    for h in order:
        nbr_copy(h % CHIPS).start()
    weights_step(4)
    weights("slabs_on", 4)
    weights("slabs_out", 5, 6)
    weights("pieces_out", 7)
    tok[0].step(4)
    weights("pieces_on", 7)
    tok[1].step(4)
    for t in tok:
        for h in range(CHIPS):
            t.from_sibling(z + h)
    weights("slabs_out", 7)
    load_dec.wait()
    make_cond(0)
    weights("slabs_on", 5)
    make_cond(1)
    weights("slabs_on", 6)
    r.qpad[pl.ds(1, CHIPS * GROUP), :] = project(0).astype(BF16).astype(F32)
    r.hq[...] = r.qpad[pl.ds(0, GROUP), :].astype(BF16)
    send_q.start()
    weights("slabs_on", 7)
    for h in order:
        nbr_arrived(h)
    nbr_sib.start()
    nbr_sib_in.wait_recv()
    lax.fori_loop(0, CHIPS, encode, 0)

    r.sum_out[...] = of_slot(r.enc_sum[...], 1 - core).astype(BF16)
    sum_copy.start()
    raw = of_slot(r.nbr_all[...].astype(F32).reshape(2 * NLEN, enc_width), core)
    mine = raw + of_slot(r.enc_sum[...], core)
    sum_copy.wait_recv()
    combined = mine + r.sum_got[...].astype(F32)
    factor = lax.rsqrt(jnp.mean(combined * combined, axis=-1, keepdims=True) + 1e-06)
    encoded = (combined * factor * r.gain[...].reshape(1, enc_width)).astype(BF16)
    for k in range(2):
        r.enc_all[k, p.me] = encoded[half_rows * k : half_rows * (k + 1)]
        enc[k].own()
    r.enc_ref[...] = encoded
    send_q.wait_recv()
    load_out.wait()
    for h in (1, 2):
        for k in range(2):
            enc[k].step(h)
    for h in (0, 1, -1, 2, -2):
        enc[0].from_sibling(z + h)

    def first_kv(i, _):
        make_kv(0, p.nth(i))
        return 0

    lax.fori_loop(0, 5, first_kv, 0)
    for h in (0, 1, -1):
        enc[1].from_sibling(z + h)
    attend_all(0, 3)
    enc[0].step(3)
    enc[1].step(3)
    make_outs((z, z + 1))
    for h in (2, -2):
        enc[1].from_sibling(z + h)
    attend_all(3, 2)
    enc[0].step(4)
    enc[1].step(4)
    make_outs((z - 1, z + 2))
    for h in (3, -3, 4):
        enc[0].from_sibling(z + h)
    lax.fori_loop(5, CHIPS, first_kv, 0)
    for h in (3, -3):
        enc[1].from_sibling(z + h)
    attend_all(5, 2)
    enc[1].from_sibling(z + 4)
    attend_all(7, 1)
    make_outs((z + 4,))
    for k in range(2):
        out_sum.item(k, jnp.int32(0))
    make_outs((z - 3, z + 3, z - 2))

    def out_items(i, _):
        for k in range(2):
            out_sum.item(k, i)
        return 0

    lax.fori_loop(1, CHIPS - 1, out_items, 0)
    for k in range(2):
        r.out_ref[:, pl.ds(k * half_model, half_model)] = out_sum.total(k).astype(BF16)

    for g in (*tok, *enc, *weights_z, *weights_xy):
        g.drain()
    out_sum.drain()
    for h in range(1, CHIPS):
        nbr_copy(h).wait_send()
        for j in range(2):
            cond_copy(j, h).wait_send()
    for c in (nbr_sib, sum_copy, send_q, send_a):
        c.wait_send()


def local(
    tokens, nbr_embed, neighbour_table, valid_counts, dec_proj, enc_query, enc_out, enc_gain, nbr_proj, out_proj
):
    rows, model = tokens.shape
    nbrs, piece, enc_width = nbr_embed.shape
    width = enc_query.shape[1]
    block = 2 * piece
    sub = NLEN // 2
    padded = GROUP * (CHIPS + 1) + 8
    dma = pltpu.SemaphoreType.DMA
    half = (rows, model // 2)
    scratch = {
        "tok_all": pltpu.VMEM((2, 16, *half), BF16),
        "enc_all": pltpu.VMEM((2, 16, sub, enc_width), BF16),
        "nbr_all": pltpu.VMEM((CHIPS, 2, block, enc_width), BF16),
        "nbr_send": pltpu.VMEM((CHIPS, block, enc_width), BF16),
        "nbr_raw": pltpu.VMEM((nbrs, piece, enc_width), BF16),
        "nbr32": pltpu.VMEM((nbrs, piece, enc_width), F32),
        "wdec": pltpu.VMEM((3, model, width), BF16),
        "wq_all": pltpu.VMEM((CHIPS, enc_width, width), BF16),
        "wo_all": pltpu.VMEM((CHIPS, width, enc_width), BF16),
        "wkv_raw": pltpu.VMEM((enc_width, 2, width), BF16),
        "wkv": pltpu.VMEM((2, enc_width, width), BF16),
        "wout": pltpu.VMEM((width, model), BF16),
        "qpad": pltpu.VMEM((padded, width), F32),
        "cond": pltpu.VMEM((2, GROUP * CHIPS, width), BF16),
        "cond_got": pltpu.VMEM((CHIPS, 2, GROUP, width), BF16),
        "enc_sum": pltpu.VMEM((2 * NLEN, enc_width), F32),
        "sum_out": pltpu.VMEM((NLEN, enc_width), BF16),
        "sum_got": pltpu.VMEM((NLEN, enc_width), BF16),
        "kv": pltpu.VMEM((2, CHIPS, 2 * NLEN, width), BF16),
        "att": pltpu.VMEM((padded, width), F32),
        "opart": pltpu.VMEM((2, CHIPS, 2, *half), BF16),
        "osib": pltpu.VMEM((2, CHIPS, *half), BF16),
        "obox": pltpu.VMEM((2, CHIPS + 1, *half), BF16),
        "oout": pltpu.VMEM((2, CHIPS - 1, *half), BF16),
        **{name: pltpu.VMEM((GROUP, width), BF16) for name in ("hq", "hq_got", "ha", "ha_got")},
        "load_sems": dma((8,)),
        "halo_sems": dma((4,)),
        "nbr_sems": dma((2, CHIPS)),
        "pair_sems": dma((4,)),
        "cond_s": dma((2, CHIPS)),
        "cond_r": dma((2, CHIPS)),
        **{f"{name}_{x}": dma((2, n)) for name in ("tok", "enc", "wz") for x, n in (("f", 7), ("s", 8), ("r", 16))},
        **{f"x{c}": dma((2, CHIPS, 2)) if c in "abef" else dma((2, CHIPS)) for c in "abcdefgh"},
        **{f"o{j}": dma((2, n)) for j, n in enumerate((8, 8, 7, 9))},
    }
    inputs = {
        "tok_in": (tokens, pl.ANY),
        "nbr_in": (nbr_embed, pl.ANY),
        "table": (neighbour_table.T, pltpu.SMEM),
        "counts": (valid_counts, pltpu.SMEM),
        "dec_in": (jnp.transpose(dec_proj, (1, 0, 2)), pl.ANY),
        "wq_in": (enc_query, pl.ANY),
        "wo_in": (enc_out, pl.ANY),
        "gain": (enc_gain, pltpu.VMEM),
        "wkv_in": (nbr_proj, pl.ANY),
        "wout_in": (out_proj, pl.ANY),
    }
    vmem = pl.BlockSpec(memory_space=pltpu.VMEM)
    names = (*inputs, "out_ref", "enc_ref", *scratch)
    return pl.pallas_call(
        functools.partial(kernel, names),
        out_shape=(
            jax.ShapeDtypeStruct((rows, model), BF16),
            jax.ShapeDtypeStruct((NLEN, enc_width), BF16),
        ),
        in_specs=[pl.BlockSpec(memory_space=space) for _, space in inputs.values()],
        out_specs=(vmem, vmem),
        scratch_shapes=list(scratch.values()),
        compiler_params=pltpu.CompilerParams(
            collective_id=0, has_side_effects=True, vmem_limit_bytes=60 * 2**20
        ),
        name="retrieval",
    )(*(array for array, _ in inputs.values()))


def solution(mesh):
    return jax.shard_map(
        local,
        mesh=mesh,
        in_specs=(
            P(("seq", "nbr"), None),
            P("seq", "nbr", None),
            P("seq", None),
            P(),
            P(None, None, "nbr"),
            P(None, "nbr"),
            P("nbr", None),
            P(),
            P(None, None, "nbr"),
            P("nbr", None),
        ),
        out_specs=(P(("seq", "nbr"), None), P(("seq", "nbr"), None)),
        check_vma=False,
    )
```

time: 345 us -> 141 us (0.41)
  waiting for transfers between devices: 255 us -> 0 us
  Pallas kernels: 0 us -> 137 us
  local copies, waits for them, and re-layouts: 34 us -> 3.31 us
  matrix products: 23.3 us -> 0 us
  between operations: 14.1 us -> 0.64 us
  other arithmetic: 12.2 us -> 0 us
  starting transfers between devices: 3.45 us -> 0 us
    pallas_call x0 -> x1, Pallas kernels: none -> 137 us  [local(): pl.pallas_call(functools.partial(kernel, names), out_shape=(jax.ShapeDtyp...]
    psum x1 -> x0, waiting for transfers between devices: 126 us -> none  [local(): lax.psum(jnp.dot(enc_att, enc_out, preferred_element_type=jnp.float32), '...]
    all_gather x2 -> x0, waiting for transfers between devices: 68.6 us -> none  [the longest x1 37.1 us: local(): grp_embed = lax.all_gather(nbr_embed, 'nbr', axis=1, tiled=True)]
    reduce_scatter x1 -> x0, waiting for transfers between devices: 59.3 us -> none  [local(): lax.psum_scatter(jnp.dot(cca_att, out_proj, preferred_element_type=jnp.fl...]
    dot_general x9 -> x0, matrix products: 23.3 us -> none  [the longest x1 7.51 us: local(): jnp.dot(lax.all_gather(tokens, 'nbr', axis=0, tiled=True), dec_flat, pref...]
    unnamed x31 -> x2, local copies, waits for them, and re-layouts: 15.5 us -> 3.31 us
    concatenate x5 -> x0, local copies, waits for them, and re-layouts: 6.36 us -> none  [the longest x3 6.28 us: local(): kv_ext = jnp.concatenate([previous[None], nbr_kv], axis=0)]
    reduce_sum x2 -> x0, other arithmetic: 5.97 us -> none  [the longest x1 5.5 us: normed_rows(): jnp.mean(combined * combined, axis=-1, keepdims=True) + 1e-06]
  transfers between devices with their start and end apart: 5 -> 0, of which waited for: 4 -> 0; matrix products, arithmetic and copies ran while one was open for 8% -> 0% of each run, Pallas kernels for 0% -> 0%
where the time goes in v2:
time: 141 us
  Pallas kernels  137 us (97%)
  local copies, waits for them, and re-layouts  3.31 us (2%)
    pallas_call x1, Pallas kernels, local(): pl.pallas_call(functools.partial(kernel, names), out_shape=(jax.ShapeDtyp...  137 us
    unnamed x2, local copies, waits for them, and re-layouts  3.31 us

profile of v2, /device:TPU:1, one launch (start us, length us, event | category | flops | bytes accessed | tf_op | source)
XLA Modules:
  0.0 141.3 jit_solution(2086481763128615818)
XLA Ops:
  0.6 137.3 %retrieval.1 = (bf16[32,4096]{1,0:T(8,128)(2,1)}, bf16[128,896]{1,0:T(8,128)(2,1)}) custom-call(bf16[32,4096]{1,0:T(8,128)(2,1)} %refs_0_.1, bf16[16,8,896]{2,1,0:T(8,128)(2,1)} %refs_1_.1, s32[2,8]{1,0:T(2,128)} %bitcast.3, s32[128]{0:T(128)} %refs_3_.1, bf16[3,4096,256]{2,1,0:T(8,128)(2,1)} %bitcast.2, bf16[896,256]{1,0:T(8,128)(2,1)} %refs_5_.1, ...), custom_call_target="tpu_custom_call" | custom-call | tf_op jit(solution)/shard_map/retrieval/pallas_call | solution.py:676
  138.0 1.7 %copy.14 = bf16[32,4096]{1,0:T(8,128)(2,1)} copy(bf16[32,4096]{1,0:T(8,128)(2,1)} %get-tuple-element.4) | data formatting | bytes 524288
  139.7 1.6 %copy.15 = bf16[128,896]{1,0:T(8,128)(2,1)} copy(bf16[128,896]{1,0:T(8,128)(2,1)} %get-tuple-element.5) | data formatting | bytes 458752

commit v3 on v2

--- a/solution.py
+++ b/solution.py
@@ -358,14 +358,13 @@
     )
 
     def cond_copy(j, h):
-        mine = pl.ds(pl.multiple_of(GROUP * wrap(z + h), GROUP), GROUP)
         return remote(
-            r.cond.at[j, mine], r.cond_got.at[z, j], p.on(z + h), r.cond_s.at[j, h], r.cond_r.at[j, z]
+            r.cond.at[j, wrap(z + h)], r.cond_got.at[z, j], p.on(z + h), r.cond_s.at[j, h], r.cond_r.at[j, z]
         )
 
     def cond_arrived(j, chip):
         remote(
-            r.cond.at[j, pl.ds(0, GROUP)], r.cond_got.at[chip, j], p.on(chip), r.cond_s.at[j, 0], r.cond_r.at[j, chip]
+            r.cond.at[j, 0], r.cond_got.at[chip, j], p.on(chip), r.cond_s.at[j, 0], r.cond_r.at[j, chip]
         ).wait_recv()
 
     order = (1, -1, 2, -2, 3, -3, 4)
@@ -374,39 +373,47 @@
         x0, x1 = (r.tok_all[k].reshape(CHIPS * GROUP, half_model) for k in range(2))
         return dot(x0, r.wdec[j, pl.ds(0, half_model)]) + dot(x1, r.wdec[j, pl.ds(half_model, half_model)])
 
-    def make_cond(j):
-        r.cond[j] = project(1 + j).astype(BF16)
-        for h in order:
-            cond_copy(j, h % CHIPS).start()
-        r.cond_got[z, j] = r.cond[j, pl.ds(pl.multiple_of(GROUP * z, GROUP), GROUP)]
-
-    def encode(i, _):
-        chip = p.nth(i)
-
-        @pl.when(i >= 1)
-        def _():
-            for j in range(2):
-                cond_arrived(j, chip)
-            for w in weights_xy:
-                w.ready(i)
-
-        queries = dot(r.nbr_all[...].reshape(2 * NLEN, enc_width), r.wq_all[chip]).astype(BF16)
-        per_head = []
-        for h in range(heads):
-            cols = slice(HEAD_DIM * h, HEAD_DIM * (h + 1))
-            shares = softmax(dot_t(queries[:, cols], r.cond_got[chip, 0, :, cols]) * scale)
-            per_head.append(dot(shares, r.cond_got[chip, 1, :, cols]).astype(BF16))
-        term = dot(jnp.concatenate(per_head, axis=1), r.wo_all[chip])
-
-        @pl.when(i == 0)
-        def _():
+    def make_cond(*shifts):
+        chips = [wrap(z + h) for h in shifts]
+        for t in tok:
+            for c in chips:
+                t.from_sibling(c)
+        x = [
+            jnp.concatenate([r.tok_all[k, pl.ds(2 * c, 2)].reshape(GROUP, half_model) for c in chips], axis=0)
+            for k in range(2)
+        ]
+        for j in range(2):
+            y = sum(dot(x[k], r.wdec[1 + j, pl.ds(k * half_model, half_model)]) for k in range(2)).astype(BF16)
+            for n, (h, c) in enumerate(zip(shifts, chips, strict=True)):
+                part = y[GROUP * n : GROUP * (n + 1)]
+                if h == 0:
+                    r.cond_got[z, j] = part
+                else:
+                    r.cond[j, c] = part
+                    cond_copy(j, h % CHIPS).start()
+
+    def encode(*items):
+        chips = [p.nth(i) for i in items]
+        for i, chip in zip(items, chips, strict=True):
+            if i > 0:
+                for j in range(2):
+                    cond_arrived(j, chip)
+                for w in weights_xy:
+                    w.ready(i)
+        rows = r.nbr_all[...].reshape(2 * NLEN, enc_width)
+        term = 0.0
+        for chip in chips:
+            queries = dot(rows, r.wq_all[chip]).astype(BF16)
+            per_head = []
+            for h in range(heads):
+                cols = slice(HEAD_DIM * h, HEAD_DIM * (h + 1))
+                shares = softmax(dot_t(queries[:, cols], r.cond_got[chip, 0, :, cols]) * scale)
+                per_head.append(dot(shares, r.cond_got[chip, 1, :, cols]).astype(BF16))
+            term += dot(jnp.concatenate(per_head, axis=1), r.wo_all[chip])
+        if 0 in items:
             r.enc_sum[...] = term
-
-        @pl.when(i >= 1)
-        def _():
+        else:
             r.enc_sum[...] += term
-
-        return 0
 
     def of_slot(rows, slot):
         rows = rows.reshape(16, 2, 8, enc_width)
@@ -492,55 +499,57 @@
 
     for g in (*weights_z, *tok):
         g.own()
+    weights_step(1)
+    weights("pieces_out", 1, 2)
     load_kv.wait()
     split_kv()
-    weights_step(1)
-    weights("pieces_out", 1, 2)
+    weights_step(2)
+    weights("pieces_out", 3, 4)
+    weights("pieces_on", 1, 2)
     tok[0].step(1)
-    weights("pieces_on", 1, 2)
     tok[1].step(1)
-    weights_step(2)
+    weights_step(3)
+    weights("pieces_out", 5, 6)
     weights("slabs_out", 1, 2)
-    weights("pieces_out", 3, 4)
-    tok[0].step(2)
     weights("pieces_on", 3, 4)
-    weights("slabs_on", 1)
-    tok[1].step(2)
-    weights_step(3)
-    weights("slabs_on", 2)
-    weights("slabs_out", 3, 4)
-    weights("pieces_out", 5, 6)
-    tok[0].step(3)
+    weights_step(4)
+    weights("pieces_out", 7)
+    weights("slabs_out", 3)
     weights("pieces_on", 5, 6)
-    weights("slabs_on", 3)
-    tok[1].step(3)
     for h in order:
         nbr_copy(h % CHIPS).start()
-    weights_step(4)
-    weights("slabs_on", 4)
-    weights("slabs_out", 5, 6)
-    weights("pieces_out", 7)
-    tok[0].step(4)
-    weights("pieces_on", 7)
-    tok[1].step(4)
-    for t in tok:
-        for h in range(CHIPS):
-            t.from_sibling(z + h)
-    weights("slabs_out", 7)
     load_dec.wait()
     make_cond(0)
-    weights("slabs_on", 5)
-    make_cond(1)
-    weights("slabs_on", 6)
-    r.qpad[pl.ds(1, CHIPS * GROUP), :] = project(0).astype(BF16).astype(F32)
-    r.hq[...] = r.qpad[pl.ds(0, GROUP), :].astype(BF16)
-    send_q.start()
-    weights("slabs_on", 7)
+    tok[0].step(2)
+    tok[1].step(2)
+    weights("slabs_on", 1)
+    weights("slabs_out", 4)
+    weights("pieces_on", 7)
+    weights("slabs_on", 2)
+    weights("slabs_out", 5)
+    make_cond(1, -1)
+    tok[0].step(3)
+    tok[1].step(3)
+    weights("slabs_on", 3)
+    weights("slabs_out", 6)
+    make_cond(2, -2)
+    weights("slabs_on", 4)
+    weights("slabs_out", 7)
     for h in order:
         nbr_arrived(h)
     nbr_sib.start()
+    tok[0].step(4)
+    tok[1].step(4)
+    make_cond(3, -3)
+    make_cond(4)
+    weights("slabs_on", 5)
     nbr_sib_in.wait_recv()
-    lax.fori_loop(0, CHIPS, encode, 0)
+    encode(0, 1, 2)
+    weights("slabs_on", 6)
+    encode(3, 4)
+    weights("slabs_on", 7)
+    encode(5, 6)
+    encode(7)
 
     r.sum_out[...] = of_slot(r.enc_sum[...], 1 - core).astype(BF16)
     sum_copy.start()
@@ -554,11 +563,14 @@
         r.enc_all[k, p.me] = encoded[half_rows * k : half_rows * (k + 1)]
         enc[k].own()
     r.enc_ref[...] = encoded
-    send_q.wait_recv()
+    r.qpad[pl.ds(1, CHIPS * GROUP), :] = project(0).astype(BF16).astype(F32)
+    r.hq[...] = r.qpad[pl.ds(0, GROUP), :].astype(BF16)
+    send_q.start()
     load_out.wait()
     for h in (1, 2):
         for k in range(2):
             enc[k].step(h)
+    send_q.wait_recv()
     for h in (0, 1, -1, 2, -2):
         enc[0].from_sibling(z + h)
 
@@ -637,7 +649,7 @@
         "wkv": pltpu.VMEM((2, enc_width, width), BF16),
         "wout": pltpu.VMEM((width, model), BF16),
         "qpad": pltpu.VMEM((padded, width), F32),
-        "cond": pltpu.VMEM((2, GROUP * CHIPS, width), BF16),
+        "cond": pltpu.VMEM((2, CHIPS, GROUP, width), BF16),
         "cond_got": pltpu.VMEM((CHIPS, 2, GROUP, width), BF16),
         "enc_sum": pltpu.VMEM((2 * NLEN, enc_width), F32),
         "sum_out": pltpu.VMEM((NLEN, enc_width), BF16),

time: 141 us -> 132 us (0.936)
  Pallas kernels: 137 us -> 128 us
    pallas_call x1, Pallas kernels: 137 us -> 128 us  [local(): pl.pallas_call(functools.partial(kernel, names), out_shape=(jax.ShapeDtyp...]
where the time goes in v3:
time: 132 us
  Pallas kernels  128 us (97%)
  local copies, waits for them, and re-layouts  3.31 us (3%)
    pallas_call x1, Pallas kernels, local(): pl.pallas_call(functools.partial(kernel, names), out_shape=(jax.ShapeDtyp...  128 us
    unnamed x2, local copies, waits for them, and re-layouts  3.31 us

profile of v3, /device:TPU:1, one launch (start us, length us, event | category | flops | bytes accessed | tf_op | source)
XLA Modules:
  0.0 132.0 jit_solution(4051760276956091066)
XLA Ops:
  0.6 128.1 %retrieval.1 = (bf16[32,4096]{1,0:T(8,128)(2,1)}, bf16[128,896]{1,0:T(8,128)(2,1)}) custom-call(bf16[32,4096]{1,0:T(8,128)(2,1)} %refs_0_.1, bf16[16,8,896]{2,1,0:T(8,128)(2,1)} %refs_1_.1, s32[2,8]{1,0:T(2,128)} %bitcast.3, s32[128]{0:T(128)} %refs_3_.1, bf16[3,4096,256]{2,1,0:T(8,128)(2,1)} %bitcast.2, bf16[896,256]{1,0:T(8,128)(2,1)} %refs_5_.1, ...), custom_call_target="tpu_custom_call" | custom-call | tf_op jit(solution)/shard_map/retrieval/pallas_call | solution.py:688
  128.7 1.7 %copy.14 = bf16[32,4096]{1,0:T(8,128)(2,1)} copy(bf16[32,4096]{1,0:T(8,128)(2,1)} %get-tuple-element.4) | data formatting | bytes 524288
  130.4 1.6 %copy.15 = bf16[128,896]{1,0:T(8,128)(2,1)} copy(bf16[128,896]{1,0:T(8,128)(2,1)} %get-tuple-element.5) | data formatting | bytes 458752

commit v4 on v3

--- a/solution.py
+++ b/solution.py
@@ -419,7 +419,10 @@
         rows = rows.reshape(16, 2, 8, enc_width)
         return jnp.where(slot == 0, rows[:, 0], rows[:, 1]).reshape(NLEN, enc_width)
 
-    sum_copy = remote(r.sum_out, r.sum_got, {"nbr": p.sibling}, r.pair_sems.at[2], r.pair_sems.at[3])
+    def sum_copy(k):
+        sems = r.pair_sems.at[2 + 2 * k], r.pair_sems.at[3 + 2 * k]
+        return remote(r.sum_out.at[k], r.sum_got.at[k], {"nbr": p.sibling}, *sems)
+
 
     def split_kv():
         step = 128
@@ -433,38 +436,35 @@
 
         lax.fori_loop(0, enc_width // step, body, 0)
 
-    def make_kv(k, g):
-        rows = r.enc_all[k, pl.ds(2 * g, 2)].reshape(NLEN, enc_width)
-        for j in range(2):
-            r.kv[j, g, pl.ds(NLEN * k, NLEN)] = dot(rows, r.wkv[j]).astype(BF16)
-
-    def attend(g):
-        queries = r.qpad[pl.ds(pl.multiple_of(GROUP * (g + 1), GROUP), GROUP), :]
-        own = (lax.broadcasted_iota(jnp.int32, queries.shape, 0) == 0) | (g != CHIPS - 1)
-        queries = jnp.where(own, queries, r.hq_got[...].astype(F32)).astype(BF16)
-        count = r.counts[p.seq * CHIPS + g]
+    def attend(*shifts):
+        groups = [wrap(z + h) for h in shifts]
+        for h in shifts:
+            for k in range(2):
+                enc[k].from_sibling(z + h)
         key = lax.broadcasted_iota(jnp.int32, (GROUP, 2 * NLEN), 1)
-        live = lax.rem(key // half_rows, 2) < count
-        per_head = []
-        for h in range(heads):
-            cols = slice(HEAD_DIM * h, HEAD_DIM * (h + 1))
-            scores = jnp.where(live, dot_t(queries[:, cols], r.kv[0, g, :, cols]) * scale, -1e30)
-            per_head.append(dot(softmax(scores), r.kv[1, g, :, cols]))
-        got = jnp.concatenate(per_head, axis=1).astype(BF16)
-        r.att[pl.ds(pl.multiple_of(GROUP * (g + 1), GROUP), GROUP), :] = got.astype(F32)
-
-        @pl.when(g == CHIPS - 1)
-        def _():
-            r.ha[...] = got
-            send_a.start()
-
-    def attend_all(first, count):
-        def body(i, _):
-            make_kv(1, p.nth(i))
-            attend(p.nth(i))
-            return 0
-
-        lax.fori_loop(first, first + count, body, 0)
+        slot = lax.rem(key // half_rows, 2)
+        got = []
+        for g in groups:
+            rows = r.enc_all[:, pl.ds(2 * g, 2)].reshape(2 * NLEN, enc_width)
+            keys, values = (dot(rows, r.wkv[j]).astype(BF16) for j in range(2))
+            queries = r.qpad[pl.ds(pl.multiple_of(GROUP * (g + 1), GROUP), GROUP), :]
+            own = (lax.broadcasted_iota(jnp.int32, queries.shape, 0) == 0) | (g != CHIPS - 1)
+            queries = jnp.where(own, queries, r.hq_got[...].astype(F32)).astype(BF16)
+            live = slot < r.counts[p.seq * CHIPS + g]
+            per_head = []
+            for h in range(heads):
+                cols = slice(HEAD_DIM * h, HEAD_DIM * (h + 1))
+                scores = jnp.where(live, dot_t(queries[:, cols], keys[:, cols]) * scale, -1e30)
+                per_head.append(dot(softmax(scores), values[:, cols]))
+            got.append(jnp.concatenate(per_head, axis=1).astype(BF16))
+        for g, rows in zip(groups, got, strict=True):
+            r.att[pl.ds(pl.multiple_of(GROUP * (g + 1), GROUP), GROUP), :] = rows.astype(F32)
+        for g in groups:
+
+            @pl.when(g == CHIPS - 1)
+            def _():
+                r.ha[...] = r.att[pl.ds(GROUP * CHIPS, GROUP), :].astype(BF16)
+                send_a.start()
 
     out_sum = Reduce(p, r.opart, r.osib, r.obox, r.oout, (r.o0, r.o1, r.o2, r.o3))
     half = GROUP // 2
@@ -530,86 +530,77 @@
     make_cond(1, -1)
     tok[0].step(3)
     tok[1].step(3)
+    for h in order:
+        nbr_arrived(h)
+    nbr_sib.start()
     weights("slabs_on", 3)
     weights("slabs_out", 6)
     make_cond(2, -2)
     weights("slabs_on", 4)
     weights("slabs_out", 7)
-    for h in order:
-        nbr_arrived(h)
-    nbr_sib.start()
+    nbr_sib_in.wait_recv()
+    encode(0, 1, 2)
     tok[0].step(4)
     tok[1].step(4)
     make_cond(3, -3)
     make_cond(4)
     weights("slabs_on", 5)
-    nbr_sib_in.wait_recv()
-    encode(0, 1, 2)
     weights("slabs_on", 6)
     encode(3, 4)
     weights("slabs_on", 7)
     encode(5, 6)
     encode(7)
 
-    r.sum_out[...] = of_slot(r.enc_sum[...], 1 - core).astype(BF16)
-    sum_copy.start()
-    raw = of_slot(r.nbr_all[...].astype(F32).reshape(2 * NLEN, enc_width), core)
-    mine = raw + of_slot(r.enc_sum[...], core)
-    sum_copy.wait_recv()
-    combined = mine + r.sum_got[...].astype(F32)
-    factor = lax.rsqrt(jnp.mean(combined * combined, axis=-1, keepdims=True) + 1e-06)
-    encoded = (combined * factor * r.gain[...].reshape(1, enc_width)).astype(BF16)
+    theirs = of_slot(r.enc_sum[...], 1 - core)
     for k in range(2):
-        r.enc_all[k, p.me] = encoded[half_rows * k : half_rows * (k + 1)]
+        r.sum_out[k] = theirs[half_rows * k : half_rows * (k + 1)].astype(BF16)
+        sum_copy(k).start()
+    mine = of_slot(r.nbr_all[...].astype(F32).reshape(2 * NLEN, enc_width), core) + of_slot(r.enc_sum[...], core)
+    gain = r.gain[...].reshape(1, enc_width)
+    for k in range(2):
+        sum_copy(k).wait_recv()
+        rows = slice(half_rows * k, half_rows * (k + 1))
+        combined = mine[rows] + r.sum_got[k].astype(F32)
+        factor = lax.rsqrt(jnp.mean(combined * combined, axis=-1, keepdims=True) + 1e-06)
+        encoded = (combined * factor * gain).astype(BF16)
+        r.enc_all[k, p.me] = encoded
         enc[k].own()
-    r.enc_ref[...] = encoded
+        r.enc_ref[rows] = encoded
     r.qpad[pl.ds(1, CHIPS * GROUP), :] = project(0).astype(BF16).astype(F32)
     r.hq[...] = r.qpad[pl.ds(0, GROUP), :].astype(BF16)
     send_q.start()
     load_out.wait()
-    for h in (1, 2):
+    def enc_step(h):
         for k in range(2):
             enc[k].step(h)
+
+    enc_step(1)
     send_q.wait_recv()
-    for h in (0, 1, -1, 2, -2):
-        enc[0].from_sibling(z + h)
-
-    def first_kv(i, _):
-        make_kv(0, p.nth(i))
-        return 0
-
-    lax.fori_loop(0, 5, first_kv, 0)
-    for h in (0, 1, -1):
-        enc[1].from_sibling(z + h)
-    attend_all(0, 3)
-    enc[0].step(3)
-    enc[1].step(3)
+    attend(0)
+    enc_step(2)
+    attend(1, -1)
     make_outs((z, z + 1))
-    for h in (2, -2):
-        enc[1].from_sibling(z + h)
-    attend_all(3, 2)
-    enc[0].step(4)
-    enc[1].step(4)
-    make_outs((z - 1, z + 2))
-    for h in (3, -3, 4):
-        enc[0].from_sibling(z + h)
-    lax.fori_loop(5, CHIPS, first_kv, 0)
-    for h in (3, -3):
-        enc[1].from_sibling(z + h)
-    attend_all(5, 2)
-    enc[1].from_sibling(z + 4)
-    attend_all(7, 1)
+    enc_step(3)
+    attend(2, -2)
+    attend(3, -3)
+    enc_step(4)
+    attend(4)
     make_outs((z + 4,))
-    for k in range(2):
-        out_sum.item(k, jnp.int32(0))
-    make_outs((z - 3, z + 3, z - 2))
-
-    def out_items(i, _):
-        for k in range(2):
-            out_sum.item(k, i)
-        return 0
-
-    lax.fori_loop(1, CHIPS - 1, out_items, 0)
+
+    def out_items(*items):
+        for i in items:
+            for k in range(2):
+                out_sum.item(k, jnp.int32(i))
+
+    out_items(0)
+    make_outs((z + 3, z - 3))
+    out_items(2)
+    out_items(1)
+    make_outs((z + 2, z - 2))
+    out_items(4)
+    out_items(3)
+    make_outs((z - 1,))
+    out_items(6, 5)
     for k in range(2):
         r.out_ref[:, pl.ds(k * half_model, half_model)] = out_sum.total(k).astype(BF16)
 
@@ -620,8 +611,19 @@
         nbr_copy(h).wait_send()
         for j in range(2):
             cond_copy(j, h).wait_send()
-    for c in (nbr_sib, sum_copy, send_q, send_a):
+    for c in (nbr_sib, sum_copy(0), sum_copy(1), send_q, send_a):
         c.wait_send()
+
+
+def hand_out(out_in, enc_in, out_ref, enc_ref, sems):
+    copies = [
+        pltpu.make_async_copy(out_in, out_ref, sems.at[0]),
+        pltpu.make_async_copy(enc_in, enc_ref, sems.at[1]),
+    ]
+    for c in copies:
+        c.start()
+    for c in copies:
+        c.wait()
 
 
 def local(
@@ -652,9 +654,8 @@
         "cond": pltpu.VMEM((2, CHIPS, GROUP, width), BF16),
         "cond_got": pltpu.VMEM((CHIPS, 2, GROUP, width), BF16),
         "enc_sum": pltpu.VMEM((2 * NLEN, enc_width), F32),
-        "sum_out": pltpu.VMEM((NLEN, enc_width), BF16),
-        "sum_got": pltpu.VMEM((NLEN, enc_width), BF16),
-        "kv": pltpu.VMEM((2, CHIPS, 2 * NLEN, width), BF16),
+        "sum_out": pltpu.VMEM((2, sub, enc_width), BF16),
+        "sum_got": pltpu.VMEM((2, sub, enc_width), BF16),
         "att": pltpu.VMEM((padded, width), F32),
         "opart": pltpu.VMEM((2, CHIPS, 2, *half), BF16),
         "osib": pltpu.VMEM((2, CHIPS, *half), BF16),
@@ -664,7 +665,7 @@
         "load_sems": dma((8,)),
         "halo_sems": dma((4,)),
         "nbr_sems": dma((2, CHIPS)),
-        "pair_sems": dma((4,)),
+        "pair_sems": dma((6,)),
         "cond_s": dma((2, CHIPS)),
         "cond_r": dma((2, CHIPS)),
         **{f"{name}_{x}": dma((2, n)) for name in ("tok", "enc", "wz") for x, n in (("f", 7), ("s", 8), ("r", 16))},
@@ -685,7 +686,7 @@
     }
     vmem = pl.BlockSpec(memory_space=pltpu.VMEM)
     names = (*inputs, "out_ref", "enc_ref", *scratch)
-    return pl.pallas_call(
+    results = pl.pallas_call(
         functools.partial(kernel, names),
         out_shape=(
             jax.ShapeDtypeStruct((rows, model), BF16),
@@ -699,6 +700,15 @@
         ),
         name="retrieval",
     )(*(array for array, _ in inputs.values()))
+    any_space = pl.BlockSpec(memory_space=pl.ANY)
+    return pl.pallas_call(
+        hand_out,
+        out_shape=tuple(jax.ShapeDtypeStruct(a.shape, a.dtype) for a in results),
+        in_specs=[vmem] * 2,
+        out_specs=(any_space,) * 2,
+        scratch_shapes=[dma((2,))],
+        name="hand_out",
+    )(*results)
 
 
 def solution(mesh):

time: 132 us -> 128 us (0.970)
  local copies, waits for them, and re-layouts: 3.31 us -> 0 us
    unnamed x2 -> x0, local copies, waits for them, and re-layouts: 3.31 us -> none
    pallas_call x1, Pallas kernels: 128 us -> 125 us  [local(): pl.pallas_call(functools.partial(kernel, names), out_shape=(jax.ShapeDtyp...]
    pallas_call x0 -> x1, Pallas kernels: none -> 1.81 us  [local(): pl.pallas_call(hand_out, out_shape=tuple((jax.ShapeDtypeStruct(a.shape, a...]
where the time goes in v4:
time: 128 us
  Pallas kernels  127 us (99%)
    pallas_call x1, Pallas kernels, local(): pl.pallas_call(functools.partial(kernel, names), out_shape=(jax.ShapeDtyp...  125 us

profile of v4, /device:TPU:1, one launch (start us, length us, event | category | flops | bytes accessed | tf_op | source)
XLA Modules:
  0.0 127.8 jit_solution(6016921575080296942)
XLA Ops:
  0.6 125.1 %retrieval.1 = (bf16[32,4096]{1,0:T(8,128)(2,1)}, bf16[128,896]{1,0:T(8,128)(2,1)}) custom-call(bf16[32,4096]{1,0:T(8,128)(2,1)} %refs_0_.1, bf16[16,8,896]{2,1,0:T(8,128)(2,1)} %refs_1_.1, s32[2,8]{1,0:T(2,128)} %bitcast.3, s32[128]{0:T(128)} %refs_3_.1, bf16[3,4096,256]{2,1,0:T(8,128)(2,1)} %bitcast.2, bf16[896,256]{1,0:T(8,128)(2,1)} %refs_5_.1, ...), custom_call_target="tpu_custom_call" | custom-call | tf_op jit(solution)/shard_map/retrieval/pallas_call | solution.py:689
  125.8 1.8 %hand_out.1 = (bf16[32,4096]{1,0:T(8,128)(2,1)}, bf16[128,896]{1,0:T(8,128)(2,1)}) custom-call(bf16[32,4096]{1,0:T(8,128)(2,1)} %get-tuple-element.4.out_in, bf16[128,896]{1,0:T(8,128)(2,1)} %get-tuple-element.5.enc_in), custom_call_target="tpu_custom_call" | custom-call | tf_op jit(solution)/shard_map/hand_out/pallas_call | solution.py:704

commit v5 on v4

--- a/solution.py
+++ b/solution.py
@@ -503,6 +503,8 @@
     weights("pieces_out", 1, 2)
     load_kv.wait()
     split_kv()
+    for h in order:
+        nbr_copy(h % CHIPS).start()
     weights_step(2)
     weights("pieces_out", 3, 4)
     weights("pieces_on", 1, 2)
@@ -516,8 +518,6 @@
     weights("pieces_out", 7)
     weights("slabs_out", 3)
     weights("pieces_on", 5, 6)
-    for h in order:
-        nbr_copy(h % CHIPS).start()
     load_dec.wait()
     make_cond(0)
     tok[0].step(2)
@@ -527,19 +527,20 @@
     weights("pieces_on", 7)
     weights("slabs_on", 2)
     weights("slabs_out", 5)
-    make_cond(1, -1)
-    tok[0].step(3)
-    tok[1].step(3)
     for h in order:
         nbr_arrived(h)
     nbr_sib.start()
+    make_cond(1, -1)
+    nbr_sib_in.wait_recv()
+    encode(0)
+    tok[0].step(3)
+    tok[1].step(3)
     weights("slabs_on", 3)
     weights("slabs_out", 6)
     make_cond(2, -2)
     weights("slabs_on", 4)
     weights("slabs_out", 7)
-    nbr_sib_in.wait_recv()
-    encode(0, 1, 2)
+    encode(1, 2)
     tok[0].step(4)
     tok[1].step(4)
     make_cond(3, -3)
@@ -579,7 +580,6 @@
     attend(0)
     enc_step(2)
     attend(1, -1)
-    make_outs((z, z + 1))
     enc_step(3)
     attend(2, -2)
     attend(3, -3)
@@ -599,8 +599,9 @@
     make_outs((z + 2, z - 2))
     out_items(4)
     out_items(3)
-    make_outs((z - 1,))
+    make_outs((z - 1, z + 1))
     out_items(6, 5)
+    make_outs((z,))
     for k in range(2):
         r.out_ref[:, pl.ds(k * half_model, half_model)] = out_sum.total(k).astype(BF16)
 

time: 128 us -> 123 us (0.961)
  Pallas kernels: 127 us -> 121 us
    pallas_call x1, Pallas kernels: 125 us -> 119 us  [local(): pl.pallas_call(functools.partial(kernel, names), out_shape=(jax.ShapeDtyp...]
where the time goes in v5:
time: 123 us; the launch traced here: 122 us
  Pallas kernels  121 us (98%)
    pallas_call x1, Pallas kernels, local(): pl.pallas_call(functools.partial(kernel, names), out_shape=(jax.ShapeDtyp...  119 us

profile of v5, /device:TPU:1, one launch (start us, length us, event | category | flops | bytes accessed | tf_op | source)
XLA Modules:
  0.0 122.0 jit_solution(6749044291241657082)
XLA Ops:
  0.6 119.4 %retrieval.1 = (bf16[32,4096]{1,0:T(8,128)(2,1)}, bf16[128,896]{1,0:T(8,128)(2,1)}) custom-call(bf16[32,4096]{1,0:T(8,128)(2,1)} %refs_0_.1, bf16[16,8,896]{2,1,0:T(8,128)(2,1)} %refs_1_.1, s32[2,8]{1,0:T(2,128)} %bitcast.3, s32[128]{0:T(128)} %refs_3_.1, bf16[3,4096,256]{2,1,0:T(8,128)(2,1)} %bitcast.2, bf16[896,256]{1,0:T(8,128)(2,1)} %refs_5_.1, ...), custom_call_target="tpu_custom_call" | custom-call | tf_op jit(solution)/shard_map/retrieval/pallas_call | solution.py:690
  120.1 1.8 %hand_out.1 = (bf16[32,4096]{1,0:T(8,128)(2,1)}, bf16[128,896]{1,0:T(8,128)(2,1)}) custom-call(bf16[32,4096]{1,0:T(8,128)(2,1)} %get-tuple-element.4.out_in, bf16[128,896]{1,0:T(8,128)(2,1)} %get-tuple-element.5.enc_in), custom_call_target="tpu_custom_call" | custom-call | tf_op jit(solution)/shard_map/hand_out/pallas_call | solution.py:705

commit v6 on v5

--- a/solution.py
+++ b/solution.py
@@ -582,8 +582,8 @@
     attend(1, -1)
     enc_step(3)
     attend(2, -2)
+    enc_step(4)
     attend(3, -3)
-    enc_step(4)
     attend(4)
     make_outs((z + 4,))
 

time: 123 us -> 124 us (level)
  Pallas kernels: 121 us -> 123 us
    pallas_call x1, Pallas kernels: 119 us -> 121 us  [local(): pl.pallas_call(functools.partial(kernel, names), out_shape=(jax.ShapeDtyp...]
where the time goes in v6:
time: 124 us
  Pallas kernels  123 us (99%)
    pallas_call x1, Pallas kernels, local(): pl.pallas_call(functools.partial(kernel, names), out_shape=(jax.ShapeDtyp...  121 us

profile of v6, /device:TPU:1, one launch (start us, length us, event | category | flops | bytes accessed | tf_op | source)
XLA Modules:
  0.0 123.8 jit_solution(6026111760892165942)
XLA Ops:
  0.6 121.2 %retrieval.1 = (bf16[32,4096]{1,0:T(8,128)(2,1)}, bf16[128,896]{1,0:T(8,128)(2,1)}) custom-call(bf16[32,4096]{1,0:T(8,128)(2,1)} %refs_0_.1, bf16[16,8,896]{2,1,0:T(8,128)(2,1)} %refs_1_.1, s32[2,8]{1,0:T(2,128)} %bitcast.3, s32[128]{0:T(128)} %refs_3_.1, bf16[3,4096,256]{2,1,0:T(8,128)(2,1)} %bitcast.2, bf16[896,256]{1,0:T(8,128)(2,1)} %refs_5_.1, ...), custom_call_target="tpu_custom_call" | custom-call | tf_op jit(solution)/shard_map/retrieval/pallas_call | solution.py:690
  121.8 1.8 %hand_out.1 = (bf16[32,4096]{1,0:T(8,128)(2,1)}, bf16[128,896]{1,0:T(8,128)(2,1)}) custom-call(bf16[32,4096]{1,0:T(8,128)(2,1)} %get-tuple-element.4.out_in, bf16[128,896]{1,0:T(8,128)(2,1)} %get-tuple-element.5.enc_in), custom_call_target="tpu_custom_call" | custom-call | tf_op jit(solution)/shard_map/hand_out/pallas_call | solution.py:705
